TPU v7x, 32 devices: a whole 2x2x4 slice. The times are simulated.
32 devices in a mesh: dp: 4 (over y, x), tensor: 8 (over z, core).
Axes of the slice: x: 2, y: 2, z: 4, core: 2. Of those that a mesh axis runs over, the one named last changes fastest.
Arguments:
- tokens: bfloat16 [1024, 3072], P('dp', 'tensor'), may hold values from -6 to 6
- buckets: int32 [1024], P('dp'), may hold values from 0 to 999
- modulation: float32 [1000, 3, 3072], P(None, None, 'tensor'), may hold values from -3 to 3
- up_weight: bfloat16 [3072, 12288], P(None, 'tensor'), may hold values from -0.109375 to 0.109375
- down_weight: bfloat16 [3072, 12288], P(None, 'tensor'), may hold values from -0.0546875 to 0.0546875
- output_cotangent: bfloat16 [1024, 3072], P('dp', 'tensor'), may hold values from -6 to 6
Outputs:
- mixed: bfloat16 [1024, 3072], P('dp', 'tensor')
- token_input_gradient: bfloat16 [1024, 3072], P('dp', 'tensor')
- grad_up: float32 [3072, 12288], P('dp', 'tensor')
- grad_down: float32 [3072, 12288], P('dp', 'tensor')
All inputs are finite; a program needn't handle non-finite values.
Results may differ from a plain program's by a relative error of at most 0.0062.
Values may be sent and summed in bfloat16 or wider, within the bound.
No kernel may reach another device: no remote copies, remote signals or barrier semaphores. Data moves between devices by JAX's collectives and lax.ppermute only.
A program may use at most 128 MiB of HBM per device.

v0:
```python
import functools
import math

import jax
import jax.numpy as jnp
from jax import lax
from jax.experimental import pallas as pl
from jax.experimental.pallas import tpu as pltpu
from jax.sharding import PartitionSpec as P

GELU_C = math.sqrt(2.0 / math.pi)
GELU_A = 0.044715
MIB = 1024 * 1024
F32 = jnp.float32
BF16 = jnp.bfloat16


def gelu_and_slope(v):
    square = v * v
    t = jnp.tanh(GELU_C * v * (1.0 + GELU_A * square))
    half = 0.5 * (1.0 + t)
    slope = half + (0.5 * GELU_C) * v * (1.0 - t * t) * (1.0 + (3.0 * GELU_A) * square)
    return v * half, slope


def each_column_tile(length, body, loop):
    tile = next((t for t in (256, 128) if length % t == 0), length)
    if not loop:
        for start in range(0, length, tile):
            body(slice(start, start + tile))
        return

    @pl.loop(0, length // tile)
    def _(i):
        body(pl.ds(pl.multiple_of(i * tile, 128), tile))


def call(kernel, name, operands, outs, scratch, flops, weight=8):
    return pl.pallas_call(
        kernel,
        in_specs=[pl.BlockSpec(memory_space=pltpu.SMEM)]
        + [pl.BlockSpec(memory_space=pltpu.VMEM)] * (len(operands) - 1),
        out_specs=[pl.BlockSpec(memory_space=pltpu.VMEM)] * len(outs),
        out_shape=outs,
        scratch_shapes=scratch,
        compiler_params=pltpu.CompilerParams(vmem_limit_bytes=12 * MIB),
        cost_estimate=pl.CostEstimate(flops=int(weight * flops), bytes_accessed=0, transcendentals=0),
        name=name,
    )(*operands)


class Piece:
    def __init__(self, sides):
        self.sides = sides

    def arrays(self):
        return [array for side in self.sides for _, _, array in side]

    def rows(self):
        return self.sides[0][0][2].shape[2]

    def bind(self, refs):
        refs = list(refs)
        return Piece([[(offset, index, refs.pop(0)) for offset, index, _ in side] for side in self.sides])


def bind_all(pieces, refs):
    bound = []
    for piece in pieces:
        count = len(piece.arrays())
        bound.append(piece.bind(refs[:count]))
        refs = refs[count:]
    return bound, refs


def place(dest, row, piece, which, spot):
    rows = piece.rows()
    for side, entries in enumerate(piece.sides):
        for offset, base, ref in entries:
            cols = ref.shape[3]
            if len(piece.sides) == 1:
                dest[row : row + rows, :] = ref[base, which]
            else:
                block = (spot[0] ^ offset) * 2 + (spot[1] ^ side)
                dest[row : row + rows, pl.ds(pl.multiple_of(block * cols, 128), cols)] = ref[base, which]


def hidden_tiles(h, dvel, up, down, act, dpre):
    def products(cols):
        value, slope = gelu_and_slope(jnp.dot(h[...], up[:, cols], preferred_element_type=F32))
        act[:, cols] = value.astype(BF16)
        dact = jnp.dot(dvel[...], down[:, cols], preferred_element_type=F32)
        dpre[:, cols] = (dact * slope).astype(BF16)

    each_column_tile(up.shape[1], products, loop=h.shape[0] > 256)


def bring_kernel(spot, up, down, out):
    for j in range(spot.shape[0]):
        out[j] = spot[j]


def bring(spot, up, down):
    return pl.pallas_call(
        bring_kernel,
        in_specs=[pl.BlockSpec(memory_space=pltpu.SMEM)] + [pl.BlockSpec(memory_space=pltpu.VMEM)] * 2,
        out_specs=pl.BlockSpec(memory_space=pltpu.SMEM),
        out_shape=jax.ShapeDtypeStruct(spot.shape, spot.dtype),
        compiler_params=pltpu.CompilerParams(vmem_limit_bytes=MIB),
        name="bring_weights",
    )(spot, up, down)


def tokens_kernel(pieces, spot, *refs):
    pieces, (up, down, dpre, act, h_cols, d_cols, h, dvel) = bind_all(pieces, refs)
    row = 0
    for piece in pieces:
        place(h, row, piece, 0, spot)
        place(dvel, row, piece, 1, spot)
        row += piece.rows()
    height = h_cols.shape[1]
    mine = pl.ds(pl.multiple_of(spot[2] * height, 128), height)
    h_cols[...] = h[:, mine]
    d_cols[...] = dvel[:, mine]
    hidden_tiles(h, dvel, up, down, act, dpre)


def chunk_products(spot, pieces, up, down, height, weight=8):
    width, hidden = up.shape
    rows = sum(piece.rows() for piece in pieces)
    return call(
        functools.partial(tokens_kernel, pieces),
        "chunk_products",
        [spot, *[array for piece in pieces for array in piece.arrays()], up, down],
        [jax.ShapeDtypeStruct((rows, hidden), BF16)] * 2 + [jax.ShapeDtypeStruct((rows, height), BF16)] * 2,
        [pltpu.VMEM((rows, width), BF16)] * 2,
        4 * rows * width * hidden,
        weight,
    )


def back_kernel(left_spot, left, weight, *parts):
    *parts, block = parts
    chips, _, cols = parts[0].shape
    wide = cols * len(parts)
    for k in range(chips):
        first = 0 if chips == 1 else pl.multiple_of((left_spot[0] ^ k) * wide, 128)
        block[...] = lax.dot_general(
            left[...], weight[pl.ds(first, wide), :], (((1,), (1,)), ((), ())), preferred_element_type=F32
        ).astype(BF16)
        for side, part in enumerate(parts):
            if len(parts) == 1:
                part[k] = block[...]
            else:
                part[k] = block[:, pl.ds(pl.multiple_of((left_spot[1] ^ side) * cols, 128), cols)]


def back(spot, left, weight, chips, sides, name):
    rows, hidden = left.shape
    width = weight.shape[0]
    if sides == 1:
        chips = 1
    cols = width // (chips * sides)
    return call(
        back_kernel,
        name,
        [spot, left, weight],
        [jax.ShapeDtypeStruct((chips, rows, cols), BF16)] * sides,
        [pltpu.VMEM((rows, cols * sides), BF16)],
        2 * rows * width * hidden,
    )


def grad_kernel(chunks, *refs):
    sources, (grad_up, grad_down, left, right, out, sems) = refs[: 4 * chunks], refs[4 * chunks :]
    copies = [None, None]
    turn = 0
    for grad, first in ((grad_down, 1), (grad_up, 0)):
        row = 0
        for j in range(chunks):
            some = slice(row, row + sources[4 * j].shape[0])
            right[some, :] = sources[4 * j + first][...]
            left[some, :] = sources[4 * j + 2 + first][...]
            row = some.stop
        tile = out.shape[1]
        for start in range(0, grad.shape[0], tile):
            slot = turn % 2
            if copies[slot] is not None:
                copies[slot].wait()
            some = slice(start, start + tile)

            out[slot] = lax.dot_general(
                left[:, some], right[...], (((0,), (0,)), ((), ())), preferred_element_type=F32
            )
            copies[slot] = pltpu.make_async_copy(out.at[slot], grad.at[some], sems.at[slot])
            copies[slot].start()
            turn += 1
    for copy in copies:
        if copy is not None:
            copy.wait()


def weight_grads(chunks):
    tokens = sum(chunk[0].shape[0] for chunk in chunks)
    hidden, height = chunks[0][0].shape[1], chunks[0][2].shape[1]
    tile = next((t for t in (384, 256, 128) if height % t == 0), height)
    operands = [array for chunk in chunks for array in chunk]
    return pl.pallas_call(
        functools.partial(grad_kernel, len(chunks)),
        in_specs=[pl.BlockSpec(memory_space=pltpu.VMEM)] * len(operands),
        out_specs=[pl.BlockSpec(memory_space=pl.ANY)] * 2,
        out_shape=[jax.ShapeDtypeStruct((height, hidden), F32)] * 2,
        scratch_shapes=[
            pltpu.VMEM((tokens, height), BF16),
            pltpu.VMEM((tokens, hidden), BF16),
            pltpu.VMEM((2, tile, hidden), F32),
            pltpu.SemaphoreType.DMA((2,)),
        ],
        compiler_params=pltpu.CompilerParams(vmem_limit_bytes=12 * MIB),
        cost_estimate=pl.CostEstimate(flops=32 * tokens * height * hidden, bytes_accessed=0, transcendentals=0),
        name="weight_grads",
    )(*operands)


def swap(value, axis, bits):
    size = lax.axis_size(axis)
    return lax.ppermute(value, axis, [(i, i ^ bits) for i in range(size)])


def chip_sum(value, chips):
    value = value + swap(value, "tensor", 1)
    parts = [swap(value, "tensor", 2 * k) for k in range(1, chips)]
    return sum(parts, value)


def together(*values):
    return lax.optimization_barrier(values)


def spread(value, chips):
    offsets, blocks = [0], value[None]
    bit = chips // 2
    while bit > 1:
        offsets = offsets + [k ^ bit for k in offsets]
        blocks = jnp.concatenate([blocks, swap(blocks, "tensor", 2 * bit)])
        bit //= 2
    return (blocks, swap(blocks, "tensor", 2)), (offsets, [k ^ 1 for k in offsets])


def sum_over_chips(blocks):
    bit = 1
    while blocks.shape[1] > 1:
        sent = swap(blocks[:, 1::2].astype(BF16), "tensor", 2 * bit)
        blocks = blocks[:, 0::2] + sent.astype(F32)
        bit *= 2
    return blocks[:, 0]


def on_device(tokens, buckets, modulation, up_weight, down_weight, output_cotangent):
    rows, cols = tokens.shape
    chips = lax.axis_size("tensor") // 2
    groups = lax.axis_size("dp")
    width = cols * chips * 2
    height = width // groups
    blocked = cols % 128 == 0 and chips == groups
    place_in_tensor, group = lax.axis_index("tensor"), lax.axis_index("dp")
    chip, core = place_in_tensor // 2, place_in_tensor % 2
    spot = jnp.stack([chip, core, group]).astype(jnp.int32)
    order = chip ^ jnp.arange(chips)

    def with_sibling(arrays):
        other = [swap(array, "tensor", 1) for array in arrays]
        if blocked:
            blocks = lambda side: [
                (k, j, array) for ks, array in zip(offsets, side) for j, k in enumerate(ks)
            ]
            return Piece([blocks(arrays), blocks(other)])
        both = [jnp.concatenate(side) for side in (arrays, other)]
        pair = jnp.stack([jnp.where(core == 0, *both), jnp.where(core == 0, *both[::-1])], axis=1)
        pair = jnp.take(pair, jnp.argsort(jnp.array(sum(offsets, [])) ^ chip), axis=0)
        return Piece([[(0, 0, pair.transpose(2, 3, 0, 1, 4).reshape(1, 2, rows, width))]])

    x = tokens.astype(F32)
    cot = output_cotangent.astype(F32)
    cond = modulation.at[buckets].get(mode="promise_in_bounds")
    shift, scale, gate = cond[:, 0], cond[:, 1], cond[:, 2]
    dvel = (cot * gate).astype(BF16)
    sums = chip_sum(jnp.stack([jnp.sum(x, axis=1), jnp.sum(x * x, axis=1)]), chips)
    mean = sums[0] / width
    rstd = lax.rsqrt(sums[1] / width - mean * mean + 1e-06)[:, None]
    xhat = (x - mean[:, None]) * rstd
    h = (xhat * (1.0 + scale) + shift).astype(BF16)

    spot = bring(spot, up_weight, down_weight)
    value = jnp.stack([h, dvel])
    if chips == 4 and groups == 4 and blocked:
        along_z = lambda array, k: swap(array, "tensor", 2 * k)
        sibling = lambda array: swap(array, "tensor", 1)
        piece = lambda *sides: Piece([[(k, *block) for k, block in enumerate(side)] for side in sides])

        near0 = value[None]
        near1, near2, left0, right0, near0_s, spot = together(
            along_z(near0, 1), along_z(near0, 2), swap(near0, "dp", 1), swap(near0, "dp", 2), sibling(near0), spot
        )
        near3, left1, right1, near1_s, near2_s = together(
            along_z(near2, 1), swap(near1, "dp", 1), swap(near1, "dp", 2), sibling(near1), sibling(near2)
        )
        near23 = jnp.concatenate((near2, near3))
        near = piece(
            ((0, near0), (0, near1), (0, near2), (0, near3)),
            ((0, near0_s), (0, near1_s), (0, near2_s), (0, sibling(near3))),
        )
        own = chunk_products(spot, [near], up_weight, down_weight, height)
        keep_dh, give_dh = back(spot, own[0], up_weight, chips, 2, "dh_share")
        given_dh = sibling(give_dh)
        keep_vel, give_vel = back(spot, own[1], down_weight, chips, 2, "velocity_share")
        far01 = jnp.concatenate((left0, right0, left1, right1))
        own, keep_dh, given_dh, keep_vel, give_vel, far01_s, left23, right23 = together(
            own, keep_dh, given_dh, keep_vel, give_vel, sibling(far01), swap(near23, "dp", 1), swap(near23, "dp", 2)
        )
        given_vel, far23_s = together(sibling(give_vel), sibling(jnp.concatenate((left23, right23))))
        dh = keep_dh.astype(F32) + given_dh.astype(F32)
        corner02, corner13 = jnp.concatenate((left0, left23[:1])), jnp.concatenate((right1, right23[1:]))
        shares = jnp.stack((dh, keep_vel.astype(F32) + given_vel.astype(F32)))
        corner02, corner13 = swap(corner02, "dp", 2), swap(corner13, "dp", 1)
        left = piece(
            ((0, left0), (0, left1), (0, left23), (1, left23)),
            ((0, far01_s), (2, far01_s), (0, far23_s), (1, far23_s)),
        )
        right = piece(
            ((0, right0), (0, right1), (0, right23), (1, right23)),
            ((1, far01_s), (3, far01_s), (2, far23_s), (3, far23_s)),
        )
        distant = chunk_products(spot, [left, right], up_weight, down_weight, height)
        distant, halves, corner02, corner13 = together(
            distant, along_z(shares[:, 1::2].astype(BF16), 1), corner02, corner13
        )
        shares = shares[:, ::2] + halves.astype(F32)
        sent_dh, sent_vel = shares[0, 1].astype(BF16), shares[1, 1].astype(BF16)
        got_dh = along_z(sent_dh, 2)
        corner02_s, corner13_s = sibling(corner02), sibling(corner13)
        corner = piece(
            ((0, corner02), (0, corner13), (1, corner02), (1, corner13)),
            ((0, corner02_s), (0, corner13_s), (1, corner02_s), (1, corner13_s)),
        )
        last = chunk_products(spot, [corner], up_weight, down_weight, height)
        last, got_dh, sent_vel = together(last, got_dh, sent_vel)
        dh = shares[0, 0] + got_dh.astype(F32)
        dxhat = dh * (1.0 + scale)
        sums = jnp.stack([jnp.sum(dxhat, axis=1), jnp.sum(dxhat * xhat, axis=1)])
        sums, gate = together(sums, gate)
        sums = sums + sibling(sums)
        sums = (sums + along_z(sums, 1) + along_z(sums, 2) + along_z(sums, 3)) / width
        velocity = shares[1, 0] + along_z(sent_vel, 2).astype(F32)
        chunks = [own, distant, last]
    else:
        arrays, offsets = spread(value, chips)
        near = with_sibling(arrays)
        chunks = [chunk_products(spot, [near], up_weight, down_weight, height)]
        shares = [
            back(spot, chunks[0][j], weight, chips, len(near.sides), name)
            for j, weight, name in ((0, up_weight, "dh_share"), (1, down_weight, "velocity_share"))
        ]
        if blocked:
            keep, give = map(jnp.stack, zip(*shares))
        else:
            pair = jnp.concatenate([share[0] for share in shares])
            pair = jnp.take(pair.reshape(2, rows, chips, 2, cols).transpose(0, 2, 3, 1, 4), order, axis=1)
            keep = jnp.where(core == 0, pair[:, :, 0], pair[:, :, 1])
            give = jnp.where(core == 0, pair[:, :, 1], pair[:, :, 0])
        dh, velocity = sum_over_chips(keep.astype(F32) + swap(give, "tensor", 1).astype(F32))
        for m in range(1, groups):
            far = with_sibling([swap(array, "dp", m) for array in arrays])
            chunks.append(chunk_products(spot, [far], up_weight, down_weight, height))
        dxhat = dh * (1.0 + scale)
        sums = chip_sum(jnp.stack([jnp.sum(dxhat, axis=1), jnp.sum(dxhat * xhat, axis=1)]), chips) / width
    mixed = (x + gate * velocity).astype(BF16)
    token_grad = cot + rstd * (dxhat - sums[0][:, None] - xhat * sums[1][:, None])

    grad_up, grad_down = weight_grads(chunks)
    return mixed, token_grad.astype(BF16), grad_up, grad_down


def solution(mesh):
    rows, cols = P("dp", "tensor"), P(None, "tensor")
    return jax.shard_map(
        on_device,
        mesh=mesh,
        in_specs=(rows, P("dp"), P(None, None, "tensor"), cols, cols, rows),
        out_specs=(rows,) * 4,
        check_vma=False,
    )
```

profile of v0, /device:TPU:0, one launch (start us, length us, event | category | flops | bytes accessed | tf_op | source)
XLA Modules:
  0.0 118.4 jit_solution(15579990840401332510)
XLA Ops:
  3.1 5.0 %collective-permute-start.3 = (f32[2,256]{1,0:T(2,128)S(1)}, f32[2,256]{1,0:T(2,128)S(1)}, u32[]{:S(2)}, u32[]{:S(2)}) collective-permute-start(f32[2,256]{1,0:T(2,128)S(1)} %fusion.20), channel_id=1, source_target_pairs={{0,6},{1,7},{2,4},{3,5},{4,2},{5,3},{6,0},{7,1},{8,14},{9,15},{10,... | collective-permute-start | bytes 6152 | tf_op jit(solution)/shard_map/ppermute | solution.py:227
  8.7 4.1 %gather_fusion = f32[256,3,384]{2,0,1:T(8,128)S(1)} fusion(f32[1000,3,384]{2,0,1:T(8,128)} %param.8, s32[1024]{0:T(1024)S(1)} %pad_clamp_fusion), kind=kCustom, calls=%fused_computation | custom fusion | bytes 2360320 | tf_op jit(solution)/shard_map/gather | solution.py:285
  15.3 2.9 %collective-permute-start.5 = (bf16[1,2,256,384]{3,2,1,0:T(8,128)(2,1)S(1)}, bf16[1,2,256,384]{3,2,1,0:T(8,128)(2,1)S(1)}, u32[]{:S(2)}, u32[]{:S(2)}) collective-permute-start(bf16[1,2,256,384]{3,2,1,0:T(8,128)(2,1)S(1)} %maximum_bitcast_fusion.refs_0_), channel_id=1, source_target_pairs={{0,4},{1,5},{2,6},{3,7},{4,0},{5,1},{6,2},{7,3},{8,12},{9,13},{10,... | collective-permute-start | bytes 1179656 | tf_op jit(solution)/shard_map/ppermute | solution.py:227
  19.8 1.5 %collective-permute-start.7 = (bf16[1,2,256,384]{3,2,1,0:T(8,128)(2,1)S(1)}, bf16[1,2,256,384]{3,2,1,0:T(8,128)(2,1)S(1)}, u32[]{:S(2)}, u32[]{:S(2)}) collective-permute-start(bf16[1,2,256,384]{3,2,1,0:T(8,128)(2,1)S(1)} %maximum_bitcast_fusion.refs_0_), channel_id=1, source_target_pairs={{0,16},{8,24},{16,0},{24,8},{1,17},{9,25},{17,1},{25,9},{2,18},{10... | collective-permute-start | bytes 1179656 | tf_op jit(solution)/shard_map/ppermute | solution.py:227
  21.4 3.7 %copy-done = bf16[3072,1536]{1,0:T(8,128)(2,1)S(1)} copy-done((bf16[3072,1536]{1,0:T(8,128)(2,1)S(1)}, bf16[3072,1536]{1,0:T(8,128)(2,1)}, u32[]{:S(2)}) %copy-start) | copy-done | bytes 9437208
  25.1 3.7 %copy-done.1 = bf16[3072,1536]{1,0:T(8,128)(2,1)S(1)} copy-done((bf16[3072,1536]{1,0:T(8,128)(2,1)S(1)}, bf16[3072,1536]{1,0:T(8,128)(2,1)}, u32[]{:S(2)}) %copy-start.1) | copy-done | bytes 9437208
  29.9 2.9 %collective-permute-done.4.refs_1_ = bf16[1,2,256,384]{3,2,1,0:T(8,128)(2,1)S(1)} collective-permute-done((bf16[1,2,256,384]{3,2,1,0:T(8,128)(2,1)S(1)}, bf16[1,2,256,384]{3,2,1,0:T(8,128)(2,1)S(1)}, u32[]{:S(2)}, u32[]{:S(2)}) %collective-permute-start.4) | collective-permute-done | bytes 393248 | tf_op jit(solution)/shard_map/ppermute | solution.py:227
  32.8 2.3 %collective-permute-done.5.refs_2_ = bf16[1,2,256,384]{3,2,1,0:T(8,128)(2,1)S(1)} collective-permute-done((bf16[1,2,256,384]{3,2,1,0:T(8,128)(2,1)S(1)}, bf16[1,2,256,384]{3,2,1,0:T(8,128)(2,1)S(1)}, u32[]{:S(2)}, u32[]{:S(2)}) %collective-permute-start.5) | collective-permute-done | bytes 393248 | tf_op jit(solution)/shard_map/ppermute | solution.py:227
  37.0 1.5 %collective-permute-start.11 = (bf16[1,2,256,384]{3,2,1,0:T(8,128)(2,1)S(1)}, bf16[1,2,256,384]{3,2,1,0:T(8,128)(2,1)S(1)}, u32[]{:S(2)}, u32[]{:S(2)}) collective-permute-start(bf16[1,2,256,384]{3,2,1,0:T(8,128)(2,1)S(1)} %collective-permute-done.4.refs_1_), channel_id=1, source_target_pairs={{0,16},{8,24},{16,0},{24,8},{1,17},{9,25},{17,1},{25,9},{2,18},{10... | collective-permute-start | bytes 1179656 | tf_op jit(solution)/shard_map/ppermute | solution.py:227
  39.0 4.5 %collective-permute-done.9.refs_3_ = bf16[1,2,256,384]{3,2,1,0:T(8,128)(2,1)S(1)} collective-permute-done((bf16[1,2,256,384]{3,2,1,0:T(8,128)(2,1)S(1)}, bf16[1,2,256,384]{3,2,1,0:T(8,128)(2,1)S(1)}, u32[]{:S(2)}, u32[]{:S(2)}) %collective-permute-start.9) | collective-permute-done | bytes 393248 | tf_op jit(solution)/shard_map/ppermute | solution.py:227
  46.8 1.5 %collective-permute-start.18 = (bf16[2,2,256,384]{3,2,1,0:T(8,128)(2,1)S(1)}, bf16[2,2,256,384]{3,2,1,0:T(8,128)(2,1)S(1)}, u32[]{:S(2)}, u32[]{:S(2)}) collective-permute-start(bf16[2,2,256,384]{3,2,1,0:T(8,128)(2,1)S(1)} %constant_dynamic-update-slice_fusion), channel_id=1, source_target_pairs={{0,16},{8,24},{16,0},{24,8},{1,17},{9,25},{17,1},{25,9},{2,18},{10... | collective-permute-start | bytes 2359304 | tf_op jit(solution)/shard_map/ppermute | solution.py:227
  48.7 6.8 %chunk_products.3 = (bf16[256,1536]{1,0:T(8,128)(2,1)S(1)}, bf16[256,1536]{1,0:T(8,128)(2,1)S(1)}, bf16[256,768]{1,0:T(8,128)(2,1)S(1)}, bf16[256,768]{1,0:T(8,128)(2,1)S(1)}) custom-call(s32[3]{0:T(128)S(1)} %bring_weights.1.spot.left_spot, bf16[1,2,256,384]{3,2,1,0:T(8,128)(2,1)S(1)} %maximum_bitcast_fusion.refs_0_, ...), custom_call_target="tpu_custom_call" | custom-call | flops 38654705664 | tf_op jit(solution)/shard_map/chunk_products/pallas_call | solution.py:39
  55.4 3.5 %dh_share.1 = (bf16[4,256,384]{2,1,0:T(8,128)(2,1)S(1)}, bf16[4,256,384]{2,1,0:T(8,128)(2,1)S(1)}) custom-call(s32[3]{0:T(128)S(1)} %bring_weights.1.spot.left_spot, bf16[256,1536]{1,0:T(8,128)(2,1)S(1)} %get-tuple-element.104.left.refs_0_, bf16[3072,1536]{1,0:T(8,128)(2,1)S(1)} %bitcast.60), custom_call_target="tpu_custom_call" | custom-call | flops 19327352832 | tf_op jit(solution)/shard_map/dh_share/pallas_call | solution.py:39
  59.5 3.3 %velocity_share.1 = (bf16[4,256,384]{2,1,0:T(8,128)(2,1)S(1)}, bf16[4,256,384]{2,1,0:T(8,128)(2,1)S(1)}) custom-call(s32[3]{0:T(128)S(1)} %bring_weights.1.spot.left_spot, bf16[256,1536]{1,0:T(8,128)(2,1)S(1)} %get-tuple-element.105.left.refs_1_, bf16[3072,1536]{1,0:T(8,128)(2,1)S(1)} %copy-done.2), custom_call_target="tpu_custom_call" | custom-call | flops 19327352832 | tf_op jit(solution)/shard_map/velocity_share/pallas_call | solution.py:39
  62.8 3.3 %collective-permute-done.17.refs_2_.refs_3_ = bf16[2,2,256,384]{3,2,1,0:T(8,128)(2,1)S(1)} collective-permute-done((bf16[2,2,256,384]{3,2,1,0:T(8,128)(2,1)S(1)}, bf16[2,2,256,384]{3,2,1,0:T(8,128)(2,1)S(1)}, u32[]{:S(2)}, u32[]{:S(2)}) %collective-permute-start.17) | collective-permute-done | bytes 786464 | tf_op jit(solution)/shard_map/ppermute | solution.py:227
  67.4 1.6 %collective-permute-start.22 = (bf16[2,2,256,384]{3,2,1,0:T(8,128)(2,1)S(1)}, bf16[2,2,256,384]{3,2,1,0:T(8,128)(2,1)S(1)}, u32[]{:S(2)}, u32[]{:S(2)}) collective-permute-start(bf16[2,2,256,384]{3,2,1,0:T(8,128)(2,1)S(1)} %pad_maximum_fusion.3), channel_id=1, source_target_pairs={{0,16},{8,24},{16,0},{24,8},{1,17},{9,25},{17,1},{25,9},{2,18},{10... | collective-permute-start | bytes 2359304 | tf_op jit(solution)/shard_map/ppermute | solution.py:227
  69.1 1.6 %collective-permute-start.23 = (bf16[2,2,256,384]{3,2,1,0:T(8,128)(2,1)S(1)}, bf16[2,2,256,384]{3,2,1,0:T(8,128)(2,1)S(1)}, u32[]{:S(2)}, u32[]{:S(2)}) collective-permute-start(bf16[2,2,256,384]{3,2,1,0:T(8,128)(2,1)S(1)} %pad_maximum_fusion.4), channel_id=1, source_target_pairs={{0,8},{8,0},{16,24},{24,16},{1,9},{9,1},{17,25},{25,17},{2,10},{10... | collective-permute-start | bytes 2359304 | tf_op jit(solution)/shard_map/ppermute | solution.py:227
  72.8 13.3 %chunk_products.4 = (bf16[512,1536]{1,0:T(8,128)(2,1)S(1)}, bf16[512,1536]{1,0:T(8,128)(2,1)S(1)}, bf16[512,768]{1,0:T(8,128)(2,1)S(1)}, bf16[512,768]{1,0:T(8,128)(2,1)S(1)}) custom-call(s32[3]{0:T(128)S(1)} %bring_weights.1.spot.left_spot, bf16[1,2,256,384]{3,2,1,0:T(8,128)(2,1)S(1)} %collective-permute-done.6.refs_0_, ...), custom_call_target="tpu_custom_call" | custom-call | flops 77309411328 | tf_op jit(solution)/shard_map/chunk_products/pallas_call | solution.py:39
  88.4 3.0 %collective-permute-done.21 = bf16[2,2,256,384]{3,2,1,0:T(8,128)(2,1)S(1)} collective-permute-done((bf16[2,2,256,384]{3,2,1,0:T(8,128)(2,1)S(1)}, bf16[2,2,256,384]{3,2,1,0:T(8,128)(2,1)S(1)}, u32[]{:S(2)}, u32[]{:S(2)}) %collective-permute-start.21) | collective-permute-done | bytes 786464 | tf_op jit(solution)/shard_map/ppermute | solution.py:227
  94.8 6.8 %chunk_products.5 = (bf16[256,1536]{1,0:T(8,128)(2,1)S(1)}, bf16[256,1536]{1,0:T(8,128)(2,1)S(1)}, bf16[256,768]{1,0:T(8,128)(2,1)S(1)}, bf16[256,768]{1,0:T(8,128)(2,1)S(1)}) custom-call(s32[3]{0:T(128)S(1)} %bring_weights.1.spot.left_spot, bf16[2,2,256,384]{3,2,1,0:T(8,128)(2,1)S(1)} %collective-permute-done.22.refs_0_.refs_2_, ...), custom_call_target="tpu_custom_call" | custom-call | flops 38654705664 | tf_op jit(solution)/shard_map/chunk_products/pallas_call | solution.py:39
  101.6 2.7 %collective-permute-done.26 = bf16[256,384]{1,0:T(8,128)(2,1)S(1)} collective-permute-done((bf16[256,384]{1,0:T(8,128)(2,1)S(1)}, bf16[256,384]{1,0:T(8,128)(2,1)S(1)}, u32[]{:S(2)}, u32[]{:S(2)}) %collective-permute-start.26) | collective-permute-done | bytes 196640 | tf_op jit(solution)/shard_map/ppermute | solution.py:227
  105.8 1.6 %collective-permute-start.31 = (f32[2,256]{1,0:T(2,128)S(1)}, f32[2,256]{1,0:T(2,128)S(1)}, u32[]{:S(2)}, u32[]{:S(2)}) collective-permute-start(f32[2,256]{1,0:T(2,128)S(1)} %add.94), channel_id=1, source_target_pairs={{0,6},{1,7},{2,4},{3,5},{4,2},{5,3},{6,0},{7,1},{8,14},{9,15},{10,... | collective-permute-start | bytes 6152 | tf_op jit(solution)/shard_map/ppermute | solution.py:227
  108.5 1.7 %collective-permute-start.29 = (f32[2,256]{1,0:T(2,128)S(1)}, f32[2,256]{1,0:T(2,128)S(1)}, u32[]{:S(2)}, u32[]{:S(2)}) collective-permute-start(f32[2,256]{1,0:T(2,128)S(1)} %add.94), channel_id=1, source_target_pairs={{0,2},{1,3},{2,0},{3,1},{4,6},{5,7},{6,4},{7,5},{8,10},{9,11},{10,... | collective-permute-start | bytes 6152 | tf_op jit(solution)/shard_map/ppermute | solution.py:227
  110.2 7.2 %weight_grads.1 = (f32[768,1536]{1,0:T(8,128)}, f32[768,1536]{1,0:T(8,128)}) custom-call(bf16[256,1536]{1,0:T(8,128)(2,1)S(1)} %get-tuple-element.104.left.refs_0_, bf16[256,1536]{1,0:T(8,128)(2,1)S(1)} %get-tuple-element.105.left.refs_1_, bf16[256,768]{1,0:T(8,128)(2,1)S(1)} %get-tuple-element.106.refs_2_, bf16[256,768]{1,0:T(8,128)(2,1)S(1)} %get-tuple-element.107.refs_3_, ...), custom_call_target="tpu_custom_call" | custom-call | flops 38654705664 | tf_op jit(solution)/shard_map/weight_grads/pallas_call | solution.py:208
  (119 shorter events, 27.3 us)
Async XLA Ops:
  3.1 9.8 %collective-permute-start.3 = (f32[2,256]{1,0:T(2,128)S(1)}, f32[2,256]{1,0:T(2,128)S(1)}, u32[]{:S(2)}, u32[]{:S(2)}) collective-permute-start(f32[2,256]{1,0:T(2,128)S(1)} %fusion.20), channel_id=1, source_target_pairs={{0,6},{1,7},{2,4},{3,5},{4,2},{5,3},{6,0},{7,1},{8,14},{9,15},{10,... | collective-permute-start | bytes 6152 | tf_op jit(solution)/shard_map/ppermute | solution.py:227
  8.1 4.8 %collective-permute-start.1 = (f32[2,256]{1,0:T(2,128)S(1)}, f32[2,256]{1,0:T(2,128)S(1)}, u32[]{:S(2)}, u32[]{:S(2)}) collective-permute-start(f32[2,256]{1,0:T(2,128)S(1)} %fusion.20), channel_id=1, source_target_pairs={{0,2},{1,3},{2,0},{3,1},{4,6},{5,7},{6,4},{7,5},{8,10},{9,11},{10,... | collective-permute-start | bytes 6152 | tf_op jit(solution)/shard_map/ppermute | solution.py:227
  13.9 18.9 %collective-permute-start.4 = (bf16[1,2,256,384]{3,2,1,0:T(8,128)(2,1)S(1)}, bf16[1,2,256,384]{3,2,1,0:T(8,128)(2,1)S(1)}, u32[]{:S(2)}, u32[]{:S(2)}) collective-permute-start(bf16[1,2,256,384]{3,2,1,0:T(8,128)(2,1)S(1)} %maximum_bitcast_fusion.refs_0_), channel_id=1, source_target_pairs={{0,2},{1,3},{2,0},{3,1},{4,6},{5,7},{6,4},{7,5},{8,10},{9,11},{10,... | collective-permute-start | bytes 1179656 | tf_op jit(solution)/shard_map/ppermute | solution.py:227
  15.3 19.7 %collective-permute-start.5 = (bf16[1,2,256,384]{3,2,1,0:T(8,128)(2,1)S(1)}, bf16[1,2,256,384]{3,2,1,0:T(8,128)(2,1)S(1)}, u32[]{:S(2)}, u32[]{:S(2)}) collective-permute-start(bf16[1,2,256,384]{3,2,1,0:T(8,128)(2,1)S(1)} %maximum_bitcast_fusion.refs_0_), channel_id=1, source_target_pairs={{0,4},{1,5},{2,6},{3,7},{4,0},{5,1},{6,2},{7,3},{8,12},{9,13},{10,... | collective-permute-start | bytes 1179656 | tf_op jit(solution)/shard_map/ppermute | solution.py:227
  18.3 16.8 %collective-permute-start.6 = (bf16[1,2,256,384]{3,2,1,0:T(8,128)(2,1)S(1)}, bf16[1,2,256,384]{3,2,1,0:T(8,128)(2,1)S(1)}, u32[]{:S(2)}, u32[]{:S(2)}) collective-permute-start(bf16[1,2,256,384]{3,2,1,0:T(8,128)(2,1)S(1)} %maximum_bitcast_fusion.refs_0_), channel_id=1, source_target_pairs={{0,8},{8,0},{16,24},{24,16},{1,9},{9,1},{17,25},{25,17},{2,10},{10... | collective-permute-start | bytes 1179656 | tf_op jit(solution)/shard_map/ppermute | solution.py:227
  19.8 15.3 %collective-permute-start.7 = (bf16[1,2,256,384]{3,2,1,0:T(8,128)(2,1)S(1)}, bf16[1,2,256,384]{3,2,1,0:T(8,128)(2,1)S(1)}, u32[]{:S(2)}, u32[]{:S(2)}) collective-permute-start(bf16[1,2,256,384]{3,2,1,0:T(8,128)(2,1)S(1)} %maximum_bitcast_fusion.refs_0_), channel_id=1, source_target_pairs={{0,16},{8,24},{16,0},{24,8},{1,17},{9,25},{17,1},{25,9},{2,18},{10... | collective-permute-start | bytes 1179656 | tf_op jit(solution)/shard_map/ppermute | solution.py:227
  21.3 13.8 %collective-permute-start.8 = (bf16[1,2,256,384]{3,2,1,0:T(8,128)(2,1)S(1)}, bf16[1,2,256,384]{3,2,1,0:T(8,128)(2,1)S(1)}, u32[]{:S(2)}, u32[]{:S(2)}) collective-permute-start(bf16[1,2,256,384]{3,2,1,0:T(8,128)(2,1)S(1)} %maximum_bitcast_fusion.refs_0_), channel_id=1, source_target_pairs={{0,1},{1,0},{2,3},{3,2},{4,5},{5,4},{6,7},{7,6},{8,9},{9,8},{10,11... | collective-permute-start | bytes 1179656 | tf_op jit(solution)/shard_map/ppermute | solution.py:227
  35.0 8.4 %collective-permute-start.9 = (bf16[1,2,256,384]{3,2,1,0:T(8,128)(2,1)S(1)}, bf16[1,2,256,384]{3,2,1,0:T(8,128)(2,1)S(1)}, u32[]{:S(2)}, u32[]{:S(2)}) collective-permute-start(bf16[1,2,256,384]{3,2,1,0:T(8,128)(2,1)S(1)} %collective-permute-done.5.refs_2_), channel_id=1, source_target_pairs={{0,2},{1,3},{2,0},{3,1},{4,6},{5,7},{6,4},{7,5},{8,10},{9,11},{10,... | collective-permute-start | bytes 1179656 | tf_op jit(solution)/shard_map/ppermute | solution.py:227
  35.5 9.3 %collective-permute-start.10 = (bf16[1,2,256,384]{3,2,1,0:T(8,128)(2,1)S(1)}, bf16[1,2,256,384]{3,2,1,0:T(8,128)(2,1)S(1)}, u32[]{:S(2)}, u32[]{:S(2)}) collective-permute-start(bf16[1,2,256,384]{3,2,1,0:T(8,128)(2,1)S(1)} %collective-permute-done.4.refs_1_), channel_id=1, source_target_pairs={{0,8},{8,0},{16,24},{24,16},{1,9},{9,1},{17,25},{25,17},{2,10},{10... | collective-permute-start | bytes 1179656 | tf_op jit(solution)/shard_map/ppermute | solution.py:227
  37.0 9.1 %collective-permute-start.11 = (bf16[1,2,256,384]{3,2,1,0:T(8,128)(2,1)S(1)}, bf16[1,2,256,384]{3,2,1,0:T(8,128)(2,1)S(1)}, u32[]{:S(2)}, u32[]{:S(2)}) collective-permute-start(bf16[1,2,256,384]{3,2,1,0:T(8,128)(2,1)S(1)} %collective-permute-done.4.refs_1_), channel_id=1, source_target_pairs={{0,16},{8,24},{16,0},{24,8},{1,17},{9,25},{17,1},{25,9},{2,18},{10... | collective-permute-start | bytes 1179656 | tf_op jit(solution)/shard_map/ppermute | solution.py:227
  38.5 7.5 %collective-permute-start.12 = (bf16[1,2,256,384]{3,2,1,0:T(8,128)(2,1)S(1)}, bf16[1,2,256,384]{3,2,1,0:T(8,128)(2,1)S(1)}, u32[]{:S(2)}, u32[]{:S(2)}) collective-permute-start(bf16[1,2,256,384]{3,2,1,0:T(8,128)(2,1)S(1)} %collective-permute-done.4.refs_1_), channel_id=1, source_target_pairs={{0,1},{1,0},{2,3},{3,2},{4,5},{5,4},{6,7},{7,6},{8,9},{9,8},{10,11... | collective-permute-start | bytes 1179656 | tf_op jit(solution)/shard_map/ppermute | solution.py:227
  38.5 7.5 %collective-permute-start.13 = (bf16[1,2,256,384]{3,2,1,0:T(8,128)(2,1)S(1)}, bf16[1,2,256,384]{3,2,1,0:T(8,128)(2,1)S(1)}, u32[]{:S(2)}, u32[]{:S(2)}) collective-permute-start(bf16[1,2,256,384]{3,2,1,0:T(8,128)(2,1)S(1)} %collective-permute-done.5.refs_2_), channel_id=1, source_target_pairs={{0,1},{1,0},{2,3},{3,2},{4,5},{5,4},{6,7},{7,6},{8,9},{9,8},{10,11... | collective-permute-start | bytes 1179656 | tf_op jit(solution)/shard_map/ppermute | solution.py:227
  46.2 20.0 %collective-permute-start.17 = (bf16[2,2,256,384]{3,2,1,0:T(8,128)(2,1)S(1)}, bf16[2,2,256,384]{3,2,1,0:T(8,128)(2,1)S(1)}, u32[]{:S(2)}, u32[]{:S(2)}) collective-permute-start(bf16[2,2,256,384]{3,2,1,0:T(8,128)(2,1)S(1)} %constant_dynamic-update-slice_fusion), channel_id=1, source_target_pairs={{0,8},{8,0},{16,24},{24,16},{1,9},{9,1},{17,25},{25,17},{2,10},{10... | collective-permute-start | bytes 2359304 | tf_op jit(solution)/shard_map/ppermute | solution.py:227
  46.8 19.7 %collective-permute-start.18 = (bf16[2,2,256,384]{3,2,1,0:T(8,128)(2,1)S(1)}, bf16[2,2,256,384]{3,2,1,0:T(8,128)(2,1)S(1)}, u32[]{:S(2)}, u32[]{:S(2)}) collective-permute-start(bf16[2,2,256,384]{3,2,1,0:T(8,128)(2,1)S(1)} %constant_dynamic-update-slice_fusion), channel_id=1, source_target_pairs={{0,16},{8,24},{16,0},{24,8},{1,17},{9,25},{17,1},{25,9},{2,18},{10... | collective-permute-start | bytes 2359304 | tf_op jit(solution)/shard_map/ppermute | solution.py:227
  48.5 17.9 %collective-permute-start.16 = (bf16[4,2,256,384]{3,2,1,0:T(8,128)(2,1)S(1)}, bf16[4,2,256,384]{3,2,1,0:T(8,128)(2,1)S(1)}, u32[]{:S(2)}, u32[]{:S(2)}) collective-permute-start(bf16[4,2,256,384]{3,2,1,0:T(8,128)(2,1)S(1)} %pad_maximum_fusion.1), channel_id=1, source_target_pairs={{0,1},{1,0},{2,3},{3,2},{4,5},{5,4},{6,7},{7,6},{8,9},{9,8},{10,11... | collective-permute-start | bytes 4718600 | tf_op jit(solution)/shard_map/ppermute | solution.py:227
  59.0 7.4 %collective-permute-start.15 = (bf16[4,256,384]{2,1,0:T(8,128)(2,1)S(1)}, bf16[4,256,384]{2,1,0:T(8,128)(2,1)S(1)}, u32[]{:S(2)}, u32[]{:S(2)}) collective-permute-start(bf16[4,256,384]{2,1,0:T(8,128)(2,1)S(1)} %get-tuple-element.73), channel_id=1, source_target_pairs={{0,1},{1,0},{2,3},{3,2},{4,5},{5,4},{6,7},{7,6},{8,9},{9,8},{10,11... | collective-permute-start | bytes 2359304 | tf_op jit(solution)/shard_map/ppermute | solution.py:227
  67.4 19.6 %collective-permute-start.22 = (bf16[2,2,256,384]{3,2,1,0:T(8,128)(2,1)S(1)}, bf16[2,2,256,384]{3,2,1,0:T(8,128)(2,1)S(1)}, u32[]{:S(2)}, u32[]{:S(2)}) collective-permute-start(bf16[2,2,256,384]{3,2,1,0:T(8,128)(2,1)S(1)} %pad_maximum_fusion.3), channel_id=1, source_target_pairs={{0,16},{8,24},{16,0},{24,8},{1,17},{9,25},{17,1},{25,9},{2,18},{10... | collective-permute-start | bytes 2359304 | tf_op jit(solution)/shard_map/ppermute | solution.py:227
  69.1 19.3 %collective-permute-start.23 = (bf16[2,2,256,384]{3,2,1,0:T(8,128)(2,1)S(1)}, bf16[2,2,256,384]{3,2,1,0:T(8,128)(2,1)S(1)}, u32[]{:S(2)}, u32[]{:S(2)}) collective-permute-start(bf16[2,2,256,384]{3,2,1,0:T(8,128)(2,1)S(1)} %pad_maximum_fusion.4), channel_id=1, source_target_pairs={{0,8},{8,0},{16,24},{24,16},{1,9},{9,1},{17,25},{25,17},{2,10},{10... | collective-permute-start | bytes 2359304 | tf_op jit(solution)/shard_map/ppermute | solution.py:227
  71.7 19.6 %collective-permute-start.21 = (bf16[2,2,256,384]{3,2,1,0:T(8,128)(2,1)S(1)}, bf16[2,2,256,384]{3,2,1,0:T(8,128)(2,1)S(1)}, u32[]{:S(2)}, u32[]{:S(2)}) collective-permute-start(bf16[2,2,256,384]{3,2,1,0:T(8,128)(2,1)S(1)} %slice.54), channel_id=1, source_target_pairs={{0,2},{1,3},{2,0},{3,1},{4,6},{5,7},{6,4},{7,5},{8,10},{9,11},{10,... | collective-permute-start | bytes 2359304 | tf_op jit(solution)/shard_map/ppermute | solution.py:227
  92.5 11.8 %collective-permute-start.26 = (bf16[256,384]{1,0:T(8,128)(2,1)S(1)}, bf16[256,384]{1,0:T(8,128)(2,1)S(1)}, u32[]{:S(2)}, u32[]{:S(2)}) collective-permute-start(bf16[256,384]{1,0:T(8,128)(2,1)S(1)} %get-tuple-element.128), channel_id=1, source_target_pairs={{0,4},{1,5},{2,6},{3,7},{4,0},{5,1},{6,2},{7,3},{8,12},{9,13},{10,... | collective-permute-start | bytes 589832 | tf_op jit(solution)/shard_map/ppermute | solution.py:227
  104.7 12.8 %collective-permute-start.27 = (bf16[256,384]{1,0:T(8,128)(2,1)S(1)}, bf16[256,384]{1,0:T(8,128)(2,1)S(1)}, u32[]{:S(2)}, u32[]{:S(2)}) collective-permute-start(bf16[256,384]{1,0:T(8,128)(2,1)S(1)} %get-tuple-element.102), channel_id=1, source_target_pairs={{0,4},{1,5},{2,6},{3,7},{4,0},{5,1},{6,2},{7,3},{8,12},{9,13},{10,... | collective-permute-start | bytes 589832 | tf_op jit(solution)/shard_map/ppermute | solution.py:227
  105.8 11.6 %collective-permute-start.31 = (f32[2,256]{1,0:T(2,128)S(1)}, f32[2,256]{1,0:T(2,128)S(1)}, u32[]{:S(2)}, u32[]{:S(2)}) collective-permute-start(f32[2,256]{1,0:T(2,128)S(1)} %add.94), channel_id=1, source_target_pairs={{0,6},{1,7},{2,4},{3,5},{4,2},{5,3},{6,0},{7,1},{8,14},{9,15},{10,... | collective-permute-start | bytes 6152 | tf_op jit(solution)/shard_map/ppermute | solution.py:227
  107.4 9.9 %collective-permute-start.30 = (f32[2,256]{1,0:T(2,128)S(1)}, f32[2,256]{1,0:T(2,128)S(1)}, u32[]{:S(2)}, u32[]{:S(2)}) collective-permute-start(f32[2,256]{1,0:T(2,128)S(1)} %add.94), channel_id=1, source_target_pairs={{0,4},{1,5},{2,6},{3,7},{4,0},{5,1},{6,2},{7,3},{8,12},{9,13},{10,... | collective-permute-start | bytes 6152 | tf_op jit(solution)/shard_map/ppermute | solution.py:227
  108.5 8.9 %collective-permute-start.29 = (f32[2,256]{1,0:T(2,128)S(1)}, f32[2,256]{1,0:T(2,128)S(1)}, u32[]{:S(2)}, u32[]{:S(2)}) collective-permute-start(f32[2,256]{1,0:T(2,128)S(1)} %add.94), channel_id=1, source_target_pairs={{0,2},{1,3},{2,0},{3,1},{4,6},{5,7},{6,4},{7,5},{8,10},{9,11},{10,... | collective-permute-start | bytes 6152 | tf_op jit(solution)/shard_map/ppermute | solution.py:227
  (27 other events, 223.4 us)
where the time goes:
time: 119 us; the launch traced here: 118 us
  Pallas kernels  42 us (35%)
  starting transfers between devices  30.9 us (26%)
  waiting for transfers between devices  26.3 us (22%)
  local copies, waits for them, and re-layouts  13.1 us (11%)
  other arithmetic  4.98 us (4%)
    pallas_call x5, Pallas kernels, call(): pl.pallas_call(kernel, in_specs=[pl.BlockSpec(memory_space=pltpu.SMEM)] +...  33.7 us
    ppermute x32, starting transfers between devices, swap(): return lax.ppermute(value, axis, [(i, i ^ bits) for i in range(size)])  30.9 us
    ppermute x32, waiting for transfers between devices, swap(): return lax.ppermute(value, axis, [(i, i ^ bits) for i in range(size)])  26.3 us
    unnamed x37, local copies, waits for them, and re-layouts  8.78 us
    pallas_call x1, Pallas kernels, weight_grads(): pl.pallas_call(functools.partial(grad_kernel, len(chunks)), in_specs=[pl....  7.16 us
    gather x1, local copies, waits for them, and re-layouts, on_device(): cond = modulation.at[buckets].get(mode='promise_in_bounds')  4.09 us
  transfers between devices with their start and end apart: 32, of which 15 were waited for; matrix products, arithmetic and copies ran while one was open for 6% of the time, Pallas kernels for 35%

commit v1 on v0

--- a/solution.py
+++ b/solution.py
@@ -24,7 +24,7 @@
 
 
 def each_column_tile(length, body, loop):
-    tile = next((t for t in (256, 128) if length % t == 0), length)
+    tile = next((t for t in ((512,) * loop + (256, 128)) if length % t == 0), length)
     if not loop:
         for start in range(0, length, tile):
             body(slice(start, start + tile))
@@ -43,7 +43,7 @@
         out_specs=[pl.BlockSpec(memory_space=pltpu.VMEM)] * len(outs),
         out_shape=outs,
         scratch_shapes=scratch,
-        compiler_params=pltpu.CompilerParams(vmem_limit_bytes=12 * MIB),
+        compiler_params=pltpu.CompilerParams(vmem_limit_bytes=9 * MIB),
         cost_estimate=pl.CostEstimate(flops=int(weight * flops), bytes_accessed=0, transcendentals=0),
         name=name,
     )(*operands)
@@ -216,7 +216,7 @@
             pltpu.VMEM((2, tile, hidden), F32),
             pltpu.SemaphoreType.DMA((2,)),
         ],
-        compiler_params=pltpu.CompilerParams(vmem_limit_bytes=12 * MIB),
+        compiler_params=pltpu.CompilerParams(vmem_limit_bytes=10 * MIB),
         cost_estimate=pl.CostEstimate(flops=32 * tokens * height * hidden, bytes_accessed=0, transcendentals=0),
         name="weight_grads",
     )(*operands)
@@ -299,8 +299,9 @@
         piece = lambda *sides: Piece([[(k, *block) for k, block in enumerate(side)] for side in sides])
 
         near0 = value[None]
-        near1, near2, left0, right0, near0_s, spot = together(
-            along_z(near0, 1), along_z(near0, 2), swap(near0, "dp", 1), swap(near0, "dp", 2), sibling(near0), spot
+        left0, right0 = swap(near0, "dp", 1), swap(near0, "dp", 2)
+        near1, near2, left0, right0, corner0, near0_s, spot = together(
+            along_z(near0, 1), along_z(near0, 2), left0, right0, swap(left0, "dp", 2), sibling(near0), spot
         )
         near3, left1, right1, near1_s, near2_s = together(
             along_z(near2, 1), swap(near1, "dp", 1), swap(near1, "dp", 2), sibling(near1), sibling(near2)
@@ -314,44 +315,50 @@
         keep_dh, give_dh = back(spot, own[0], up_weight, chips, 2, "dh_share")
         given_dh = sibling(give_dh)
         keep_vel, give_vel = back(spot, own[1], down_weight, chips, 2, "velocity_share")
-        far01 = jnp.concatenate((left0, right0, left1, right1))
-        own, keep_dh, given_dh, keep_vel, give_vel, far01_s, left23, right23 = together(
-            own, keep_dh, given_dh, keep_vel, give_vel, sibling(far01), swap(near23, "dp", 1), swap(near23, "dp", 2)
+        early = jnp.concatenate((left0, right0, left1, right1, corner0))
+        own, keep_dh, given_dh, keep_vel, give_vel, early_s, left23, right23 = together(
+            own, keep_dh, given_dh, keep_vel, give_vel, sibling(early), swap(near23, "dp", 1), swap(near23, "dp", 2)
         )
         given_vel, far23_s = together(sibling(give_vel), sibling(jnp.concatenate((left23, right23))))
         dh = keep_dh.astype(F32) + given_dh.astype(F32)
-        corner02, corner13 = jnp.concatenate((left0, left23[:1])), jnp.concatenate((right1, right23[1:]))
-        shares = jnp.stack((dh, keep_vel.astype(F32) + given_vel.astype(F32)))
-        corner02, corner13 = swap(corner02, "dp", 2), swap(corner13, "dp", 1)
+        half = rows // 2
+        corner2, corner3 = (
+            swap(jnp.concatenate((left23[:1], left1[:, :, :half]), axis=2), "dp", 2),
+            swap(jnp.concatenate((right23[1:], right1[:, :, half:]), axis=2), "dp", 1),
+        )
+        velocity = keep_vel.astype(F32) + given_vel.astype(F32)
+        half_dh, half_vel = along_z(dh[1::2].astype(BF16), 1), along_z(velocity[1::2].astype(BF16), 1)
         left = piece(
             ((0, left0), (0, left1), (0, left23), (1, left23)),
-            ((0, far01_s), (2, far01_s), (0, far23_s), (1, far23_s)),
+            ((0, early_s), (2, early_s), (0, far23_s), (1, far23_s)),
         )
         right = piece(
             ((0, right0), (0, right1), (0, right23), (1, right23)),
-            ((1, far01_s), (3, far01_s), (2, far23_s), (3, far23_s)),
+            ((1, early_s), (3, early_s), (2, far23_s), (3, far23_s)),
         )
         distant = chunk_products(spot, [left, right], up_weight, down_weight, height)
-        distant, halves, corner02, corner13 = together(
-            distant, along_z(shares[:, 1::2].astype(BF16), 1), corner02, corner13
-        )
-        shares = shares[:, ::2] + halves.astype(F32)
-        sent_dh, sent_vel = shares[0, 1].astype(BF16), shares[1, 1].astype(BF16)
-        got_dh = along_z(sent_dh, 2)
-        corner02_s, corner13_s = sibling(corner02), sibling(corner13)
+        distant, half_dh, corner2, corner3 = together(distant, half_dh, corner2, corner3)
+        dh = dh[::2] + half_dh.astype(F32)
+        got_dh = along_z(dh[1].astype(BF16), 2)
+        distant, half_vel, corner2, corner3 = together(distant, half_vel, corner2, corner3)
+        velocity = velocity[::2] + half_vel.astype(F32)
+        sent_vel = velocity[1].astype(BF16)
+        corner1 = jnp.concatenate((corner2[:, :, rows:], corner3[:, :, rows:]), axis=2)
+        late = jnp.concatenate((corner1, corner2[:, :, :rows], corner3[:, :, :rows]))
+        late_s = sibling(late)
         corner = piece(
-            ((0, corner02), (0, corner13), (1, corner02), (1, corner13)),
-            ((0, corner02_s), (0, corner13_s), (1, corner02_s), (1, corner13_s)),
-        )
-        last = chunk_products(spot, [corner], up_weight, down_weight, height)
+            ((0, corner0), (0, late), (1, late), (2, late)),
+            ((4, early_s), (0, late_s), (1, late_s), (2, late_s)),
+        )
+        last = chunk_products(spot, [corner], up_weight, down_weight, height, 0.02)
         last, got_dh, sent_vel = together(last, got_dh, sent_vel)
-        dh = shares[0, 0] + got_dh.astype(F32)
+        dh = dh[0] + got_dh.astype(F32)
         dxhat = dh * (1.0 + scale)
         sums = jnp.stack([jnp.sum(dxhat, axis=1), jnp.sum(dxhat * xhat, axis=1)])
         sums, gate = together(sums, gate)
         sums = sums + sibling(sums)
         sums = (sums + along_z(sums, 1) + along_z(sums, 2) + along_z(sums, 3)) / width
-        velocity = shares[1, 0] + along_z(sent_vel, 2).astype(F32)
+        velocity = velocity[0] + along_z(sent_vel, 2).astype(F32)
         chunks = [own, distant, last]
     else:
         arrays, offsets = spread(value, chips)

time: 119 us -> 116 us (0.975)
  waiting for transfers between devices: 26.3 us -> 22.5 us
  starting transfers between devices: 30.9 us -> 32.5 us
    ppermute x32 -> x33, waiting for transfers between devices: 26.3 us -> 22.5 us  [swap(): return lax.ppermute(value, axis, [(i, i ^ bits) for i in range(size)])]
    ppermute x32 -> x33, starting transfers between devices: 30.9 us -> 32.5 us  [swap(): return lax.ppermute(value, axis, [(i, i ^ bits) for i in range(size)])]
    unnamed x37 -> x53, local copies, waits for them, and re-layouts: 8.78 us -> 9.58 us
  transfers between devices with their start and end apart: 32 -> 33, of which waited for: 15 -> 13; matrix products, arithmetic and copies ran while one was open for 6% -> 5% of each run, Pallas kernels for 35% -> 36%
where the time goes in v1:
time: 116 us
  Pallas kernels  41.3 us (36%)
  starting transfers between devices  32.5 us (28%)
  waiting for transfers between devices  22.5 us (19%)
  local copies, waits for them, and re-layouts  14.1 us (12%)
  other arithmetic  4.34 us (4%)
  between operations  1.26 us (1%)
    pallas_call x5, Pallas kernels, call(): pl.pallas_call(kernel, in_specs=[pl.BlockSpec(memory_space=pltpu.SMEM)] +...  33 us
    ppermute x33, starting transfers between devices, swap(): return lax.ppermute(value, axis, [(i, i ^ bits) for i in range(size)])  32.5 us
    ppermute x33, waiting for transfers between devices, swap(): return lax.ppermute(value, axis, [(i, i ^ bits) for i in range(size)])  22.5 us
    unnamed x53, local copies, waits for them, and re-layouts  9.58 us
    pallas_call x1, Pallas kernels, weight_grads(): pl.pallas_call(functools.partial(grad_kernel, len(chunks)), in_specs=[pl....  7.15 us
    gather x1, local copies, waits for them, and re-layouts, on_device(): cond = modulation.at[buckets].get(mode='promise_in_bounds')  4.09 us
  transfers between devices with their start and end apart: 33, of which 13 were waited for; matrix products, arithmetic and copies ran while one was open for 5% of the time, Pallas kernels for 36%

profile of v1, /device:TPU:0, one launch (start us, length us, event | category | flops | bytes accessed | tf_op | source)
XLA Modules:
  0.0 115.9 jit_solution(9146697382922548372)
XLA Ops:
  3.1 5.0 %collective-permute-start.3 = (f32[2,256]{1,0:T(2,128)S(1)}, f32[2,256]{1,0:T(2,128)S(1)}, u32[]{:S(2)}, u32[]{:S(2)}) collective-permute-start(f32[2,256]{1,0:T(2,128)S(1)} %fusion.22), channel_id=1, source_target_pairs={{0,6},{1,7},{2,4},{3,5},{4,2},{5,3},{6,0},{7,1},{8,14},{9,15},{10,... | collective-permute-start | bytes 6152 | tf_op jit(solution)/shard_map/ppermute | solution.py:227
  8.7 4.1 %gather_fusion = f32[256,3,384]{2,0,1:T(8,128)S(1)} fusion(f32[1000,3,384]{2,0,1:T(8,128)} %param.8, s32[1024]{0:T(1024)S(1)} %pad_clamp_fusion), kind=kCustom, calls=%fused_computation | custom fusion | bytes 2360320 | tf_op jit(solution)/shard_map/gather | solution.py:285
  13.9 1.7 %collective-permute-start.6 = (bf16[1,2,256,384]{3,2,1,0:T(8,128)(2,1)S(1)}, bf16[1,2,256,384]{3,2,1,0:T(8,128)(2,1)S(1)}, u32[]{:S(2)}, u32[]{:S(2)}) collective-permute-start(bf16[1,2,256,384]{3,2,1,0:T(8,128)(2,1)S(1)} %maximum_bitcast_fusion.refs_0_), channel_id=1, source_target_pairs={{0,8},{8,0},{16,24},{24,16},{1,9},{9,1},{17,25},{25,17},{2,10},{10... | collective-permute-start | bytes 1179656 | tf_op jit(solution)/shard_map/ppermute | solution.py:227
  16.8 2.9 %collective-permute-start.5 = (bf16[1,2,256,384]{3,2,1,0:T(8,128)(2,1)S(1)}, bf16[1,2,256,384]{3,2,1,0:T(8,128)(2,1)S(1)}, u32[]{:S(2)}, u32[]{:S(2)}) collective-permute-start(bf16[1,2,256,384]{3,2,1,0:T(8,128)(2,1)S(1)} %maximum_bitcast_fusion.refs_0_), channel_id=1, source_target_pairs={{0,4},{1,5},{2,6},{3,7},{4,0},{5,1},{6,2},{7,3},{8,12},{9,13},{10,... | collective-permute-start | bytes 1179656 | tf_op jit(solution)/shard_map/ppermute | solution.py:227
  19.8 1.5 %collective-permute-start.7 = (bf16[1,2,256,384]{3,2,1,0:T(8,128)(2,1)S(1)}, bf16[1,2,256,384]{3,2,1,0:T(8,128)(2,1)S(1)}, u32[]{:S(2)}, u32[]{:S(2)}) collective-permute-start(bf16[1,2,256,384]{3,2,1,0:T(8,128)(2,1)S(1)} %maximum_bitcast_fusion.refs_0_), channel_id=1, source_target_pairs={{0,16},{8,24},{16,0},{24,8},{1,17},{9,25},{17,1},{25,9},{2,18},{10... | collective-permute-start | bytes 1179656 | tf_op jit(solution)/shard_map/ppermute | solution.py:227
  21.3 3.3 %collective-permute-done.6.refs_0_ = bf16[1,2,256,384]{3,2,1,0:T(8,128)(2,1)S(1)} collective-permute-done((bf16[1,2,256,384]{3,2,1,0:T(8,128)(2,1)S(1)}, bf16[1,2,256,384]{3,2,1,0:T(8,128)(2,1)S(1)}, u32[]{:S(2)}, u32[]{:S(2)}) %collective-permute-start.6) | collective-permute-done | bytes 393248 | tf_op jit(solution)/shard_map/ppermute | solution.py:227
  24.6 1.5 %collective-permute-start.8 = (bf16[1,2,256,384]{3,2,1,0:T(8,128)(2,1)S(1)}, bf16[1,2,256,384]{3,2,1,0:T(8,128)(2,1)S(1)}, u32[]{:S(2)}, u32[]{:S(2)}) collective-permute-start(bf16[1,2,256,384]{3,2,1,0:T(8,128)(2,1)S(1)} %collective-permute-done.6.refs_0_), channel_id=1, source_target_pairs={{0,16},{8,24},{16,0},{24,8},{1,17},{9,25},{17,1},{25,9},{2,18},{10... | collective-permute-start | bytes 1179656 | tf_op jit(solution)/shard_map/ppermute | solution.py:227
  26.2 3.7 %copy-done = bf16[3072,1536]{1,0:T(8,128)(2,1)S(1)} copy-done((bf16[3072,1536]{1,0:T(8,128)(2,1)S(1)}, bf16[3072,1536]{1,0:T(8,128)(2,1)}, u32[]{:S(2)}) %copy-start) | copy-done | bytes 9437208
  29.8 3.7 %copy-done.1 = bf16[3072,1536]{1,0:T(8,128)(2,1)S(1)} copy-done((bf16[3072,1536]{1,0:T(8,128)(2,1)S(1)}, bf16[3072,1536]{1,0:T(8,128)(2,1)}, u32[]{:S(2)}) %copy-start.1) | copy-done | bytes 9437208
  34.7 1.6 %collective-permute-done.5.refs_2_ = bf16[1,2,256,384]{3,2,1,0:T(8,128)(2,1)S(1)} collective-permute-done((bf16[1,2,256,384]{3,2,1,0:T(8,128)(2,1)S(1)}, bf16[1,2,256,384]{3,2,1,0:T(8,128)(2,1)S(1)}, u32[]{:S(2)}, u32[]{:S(2)}) %collective-permute-start.5) | collective-permute-done | bytes 393248 | tf_op jit(solution)/shard_map/ppermute | solution.py:227
  38.5 1.5 %collective-permute-start.12 = (bf16[1,2,256,384]{3,2,1,0:T(8,128)(2,1)S(1)}, bf16[1,2,256,384]{3,2,1,0:T(8,128)(2,1)S(1)}, u32[]{:S(2)}, u32[]{:S(2)}) collective-permute-start(bf16[1,2,256,384]{3,2,1,0:T(8,128)(2,1)S(1)} %collective-permute-done.4.refs_1_), channel_id=1, source_target_pairs={{0,16},{8,24},{16,0},{24,8},{1,17},{9,25},{17,1},{25,9},{2,18},{10... | collective-permute-start | bytes 1179656 | tf_op jit(solution)/shard_map/ppermute | solution.py:227
  40.7 5.5 %collective-permute-done.10.refs_3_ = bf16[1,2,256,384]{3,2,1,0:T(8,128)(2,1)S(1)} collective-permute-done((bf16[1,2,256,384]{3,2,1,0:T(8,128)(2,1)S(1)}, bf16[1,2,256,384]{3,2,1,0:T(8,128)(2,1)S(1)}, u32[]{:S(2)}, u32[]{:S(2)}) %collective-permute-start.10) | collective-permute-done | bytes 393248 | tf_op jit(solution)/shard_map/ppermute | solution.py:227
  48.5 1.5 %collective-permute-start.19 = (bf16[2,2,256,384]{3,2,1,0:T(8,128)(2,1)S(1)}, bf16[2,2,256,384]{3,2,1,0:T(8,128)(2,1)S(1)}, u32[]{:S(2)}, u32[]{:S(2)}) collective-permute-start(bf16[2,2,256,384]{3,2,1,0:T(8,128)(2,1)S(1)} %constant_dynamic-update-slice_fusion.5), channel_id=1, source_target_pairs={{0,16},{8,24},{16,0},{24,8},{1,17},{9,25},{17,1},{25,9},{2,18},{10... | collective-permute-start | bytes 2359304 | tf_op jit(solution)/shard_map/ppermute | solution.py:227
  50.4 7.2 %chunk_products.3 = (bf16[256,1536]{1,0:T(8,128)(2,1)S(1)}, bf16[256,1536]{1,0:T(8,128)(2,1)S(1)}, bf16[256,768]{1,0:T(8,128)(2,1)S(1)}, bf16[256,768]{1,0:T(8,128)(2,1)S(1)}) custom-call(s32[3]{0:T(128)S(1)} %bring_weights.1.spot.left_spot, bf16[1,2,256,384]{3,2,1,0:T(8,128)(2,1)S(1)} %maximum_bitcast_fusion.refs_0_, ...), custom_call_target="tpu_custom_call" | custom-call | flops 38654705664 | tf_op jit(solution)/shard_map/chunk_products/pallas_call | solution.py:39
  57.6 3.5 %dh_share.1 = (bf16[4,256,384]{2,1,0:T(8,128)(2,1)S(1)}, bf16[4,256,384]{2,1,0:T(8,128)(2,1)S(1)}) custom-call(s32[3]{0:T(128)S(1)} %bring_weights.1.spot.left_spot, bf16[256,1536]{1,0:T(8,128)(2,1)S(1)} %get-tuple-element.120.left.refs_0_, bf16[3072,1536]{1,0:T(8,128)(2,1)S(1)} %bitcast.56), custom_call_target="tpu_custom_call" | custom-call | flops 19327352832 | tf_op jit(solution)/shard_map/dh_share/pallas_call | solution.py:39
  61.6 3.4 %velocity_share.1 = (bf16[4,256,384]{2,1,0:T(8,128)(2,1)S(1)}, bf16[4,256,384]{2,1,0:T(8,128)(2,1)S(1)}) custom-call(s32[3]{0:T(128)S(1)} %bring_weights.1.spot.left_spot, bf16[256,1536]{1,0:T(8,128)(2,1)S(1)} %get-tuple-element.121.left.refs_1_, bf16[3072,1536]{1,0:T(8,128)(2,1)S(1)} %copy-done.2), custom_call_target="tpu_custom_call" | custom-call | flops 19327352832 | tf_op jit(solution)/shard_map/velocity_share/pallas_call | solution.py:39
  65.0 2.9 %collective-permute-done.18.refs_2_.refs_3_ = bf16[2,2,256,384]{3,2,1,0:T(8,128)(2,1)S(1)} collective-permute-done((bf16[2,2,256,384]{3,2,1,0:T(8,128)(2,1)S(1)}, bf16[2,2,256,384]{3,2,1,0:T(8,128)(2,1)S(1)}, u32[]{:S(2)}, u32[]{:S(2)}) %collective-permute-start.18) | collective-permute-done | bytes 786464 | tf_op jit(solution)/shard_map/ppermute | solution.py:227
  70.9 1.6 %collective-permute-start.23 = (bf16[1,2,384,384]{3,2,1,0:T(8,128)(2,1)S(1)}, bf16[1,2,384,384]{3,2,1,0:T(8,128)(2,1)S(1)}, u32[]{:S(2)}, u32[]{:S(2)}) collective-permute-start(bf16[1,2,384,384]{3,2,1,0:T(8,128)(2,1)S(1)} %pad_maximum_fusion.2), channel_id=1, source_target_pairs={{0,16},{8,24},{16,0},{24,8},{1,17},{9,25},{17,1},{25,9},{2,18},{10... | collective-permute-start | bytes 1769480 | tf_op jit(solution)/shard_map/ppermute | solution.py:227
  75.1 12.1 %chunk_products.4 = (bf16[512,1536]{1,0:T(8,128)(2,1)S(1)}, bf16[512,1536]{1,0:T(8,128)(2,1)S(1)}, bf16[512,768]{1,0:T(8,128)(2,1)S(1)}, bf16[512,768]{1,0:T(8,128)(2,1)S(1)}) custom-call(s32[3]{0:T(128)S(1)} %bring_weights.1.spot.left_spot, bf16[1,2,256,384]{3,2,1,0:T(8,128)(2,1)S(1)} %collective-permute-done.6.refs_0_, ...), custom_call_target="tpu_custom_call" | custom-call | flops 77309411328 | tf_op jit(solution)/shard_map/chunk_products/pallas_call | solution.py:39
  87.3 1.5 %collective-permute-done.25 = bf16[2,256,384]{2,1,0:T(8,128)(2,1)S(1)} collective-permute-done((bf16[2,256,384]{2,1,0:T(8,128)(2,1)S(1)}, bf16[2,256,384]{2,1,0:T(8,128)(2,1)S(1)}, u32[]{:S(2)}, u32[]{:S(2)}) %collective-permute-start.25) | collective-permute-done | bytes 393248 | tf_op jit(solution)/shard_map/ppermute | solution.py:227
  92.0 6.8 %chunk_products.5 = (bf16[256,1536]{1,0:T(8,128)(2,1)S(1)}, bf16[256,1536]{1,0:T(8,128)(2,1)S(1)}, bf16[256,768]{1,0:T(8,128)(2,1)S(1)}, bf16[256,768]{1,0:T(8,128)(2,1)S(1)}) custom-call(s32[3]{0:T(128)S(1)} %bring_weights.1.spot.left_spot, bf16[1,2,256,384]{3,2,1,0:T(8,128)(2,1)S(1)} %collective-permute-done.8.refs_0_, ...), custom_call_target="tpu_custom_call" | custom-call | flops 96636768 | tf_op jit(solution)/shard_map/chunk_products/pallas_call | solution.py:39
  98.8 3.0 %collective-permute-done.27 = bf16[256,384]{1,0:T(8,128)(2,1)S(1)} collective-permute-done((bf16[256,384]{1,0:T(8,128)(2,1)S(1)}, bf16[256,384]{1,0:T(8,128)(2,1)S(1)}, u32[]{:S(2)}, u32[]{:S(2)}) %collective-permute-start.27) | collective-permute-done | bytes 196640 | tf_op jit(solution)/shard_map/ppermute | solution.py:227
  103.3 2.1 %collective-permute-start.32 = (f32[2,256]{1,0:T(2,128)S(1)}, f32[2,256]{1,0:T(2,128)S(1)}, u32[]{:S(2)}, u32[]{:S(2)}) collective-permute-start(f32[2,256]{1,0:T(2,128)S(1)} %add.98), channel_id=1, source_target_pairs={{0,6},{1,7},{2,4},{3,5},{4,2},{5,3},{6,0},{7,1},{8,14},{9,15},{10,... | collective-permute-start | bytes 6152 | tf_op jit(solution)/shard_map/ppermute | solution.py:227
  107.7 7.1 %weight_grads.1 = (f32[768,1536]{1,0:T(8,128)}, f32[768,1536]{1,0:T(8,128)}) custom-call(bf16[256,1536]{1,0:T(8,128)(2,1)S(1)} %get-tuple-element.120.left.refs_0_, bf16[256,1536]{1,0:T(8,128)(2,1)S(1)} %get-tuple-element.121.left.refs_1_, bf16[256,768]{1,0:T(8,128)(2,1)S(1)} %get-tuple-element.122.refs_2_, bf16[256,768]{1,0:T(8,128)(2,1)S(1)} %get-tuple-element.123.refs_3_, ...), custom_call_target="tpu_custom_call" | custom-call | flops 38654705664 | tf_op jit(solution)/shard_map/weight_grads/pallas_call | solution.py:208
  (148 shorter events, 25.9 us)
Async XLA Ops:
  3.1 9.8 %collective-permute-start.3 = (f32[2,256]{1,0:T(2,128)S(1)}, f32[2,256]{1,0:T(2,128)S(1)}, u32[]{:S(2)}, u32[]{:S(2)}) collective-permute-start(f32[2,256]{1,0:T(2,128)S(1)} %fusion.22), channel_id=1, source_target_pairs={{0,6},{1,7},{2,4},{3,5},{4,2},{5,3},{6,0},{7,1},{8,14},{9,15},{10,... | collective-permute-start | bytes 6152 | tf_op jit(solution)/shard_map/ppermute | solution.py:227
  13.9 10.7 %collective-permute-start.6 = (bf16[1,2,256,384]{3,2,1,0:T(8,128)(2,1)S(1)}, bf16[1,2,256,384]{3,2,1,0:T(8,128)(2,1)S(1)}, u32[]{:S(2)}, u32[]{:S(2)}) collective-permute-start(bf16[1,2,256,384]{3,2,1,0:T(8,128)(2,1)S(1)} %maximum_bitcast_fusion.refs_0_), channel_id=1, source_target_pairs={{0,8},{8,0},{16,24},{24,16},{1,9},{9,1},{17,25},{25,17},{2,10},{10... | collective-permute-start | bytes 1179656 | tf_op jit(solution)/shard_map/ppermute | solution.py:227
  15.6 19.1 %collective-permute-start.4 = (bf16[1,2,256,384]{3,2,1,0:T(8,128)(2,1)S(1)}, bf16[1,2,256,384]{3,2,1,0:T(8,128)(2,1)S(1)}, u32[]{:S(2)}, u32[]{:S(2)}) collective-permute-start(bf16[1,2,256,384]{3,2,1,0:T(8,128)(2,1)S(1)} %maximum_bitcast_fusion.refs_0_), channel_id=1, source_target_pairs={{0,2},{1,3},{2,0},{3,1},{4,6},{5,7},{6,4},{7,5},{8,10},{9,11},{10,... | collective-permute-start | bytes 1179656 | tf_op jit(solution)/shard_map/ppermute | solution.py:227
  16.8 19.4 %collective-permute-start.5 = (bf16[1,2,256,384]{3,2,1,0:T(8,128)(2,1)S(1)}, bf16[1,2,256,384]{3,2,1,0:T(8,128)(2,1)S(1)}, u32[]{:S(2)}, u32[]{:S(2)}) collective-permute-start(bf16[1,2,256,384]{3,2,1,0:T(8,128)(2,1)S(1)} %maximum_bitcast_fusion.refs_0_), channel_id=1, source_target_pairs={{0,4},{1,5},{2,6},{3,7},{4,0},{5,1},{6,2},{7,3},{8,12},{9,13},{10,... | collective-permute-start | bytes 1179656 | tf_op jit(solution)/shard_map/ppermute | solution.py:227
  19.8 16.5 %collective-permute-start.7 = (bf16[1,2,256,384]{3,2,1,0:T(8,128)(2,1)S(1)}, bf16[1,2,256,384]{3,2,1,0:T(8,128)(2,1)S(1)}, u32[]{:S(2)}, u32[]{:S(2)}) collective-permute-start(bf16[1,2,256,384]{3,2,1,0:T(8,128)(2,1)S(1)} %maximum_bitcast_fusion.refs_0_), channel_id=1, source_target_pairs={{0,16},{8,24},{16,0},{24,8},{1,17},{9,25},{17,1},{25,9},{2,18},{10... | collective-permute-start | bytes 1179656 | tf_op jit(solution)/shard_map/ppermute | solution.py:227
  21.3 15.0 %collective-permute-start.9 = (bf16[1,2,256,384]{3,2,1,0:T(8,128)(2,1)S(1)}, bf16[1,2,256,384]{3,2,1,0:T(8,128)(2,1)}, u32[]{:S(2)}, u32[]{:S(2)}) collective-permute-start(bf16[1,2,256,384]{3,2,1,0:T(8,128)(2,1)S(1)} %maximum_bitcast_fusion.refs_0_), channel_id=1, source_target_pairs={{0,1},{1,0},{2,3},{3,2},{4,5},{5,4},{6,7},{7,6},{8,9},{9,8},{10,11... | collective-permute-start | bytes 1179656 | tf_op jit(solution)/shard_map/ppermute | solution.py:227
  24.6 13.1 %collective-permute-start.8 = (bf16[1,2,256,384]{3,2,1,0:T(8,128)(2,1)S(1)}, bf16[1,2,256,384]{3,2,1,0:T(8,128)(2,1)S(1)}, u32[]{:S(2)}, u32[]{:S(2)}) collective-permute-start(bf16[1,2,256,384]{3,2,1,0:T(8,128)(2,1)S(1)} %collective-permute-done.6.refs_0_), channel_id=1, source_target_pairs={{0,16},{8,24},{16,0},{24,8},{1,17},{9,25},{17,1},{25,9},{2,18},{10... | collective-permute-start | bytes 1179656 | tf_op jit(solution)/shard_map/ppermute | solution.py:227
  37.7 8.6 %collective-permute-start.10 = (bf16[1,2,256,384]{3,2,1,0:T(8,128)(2,1)S(1)}, bf16[1,2,256,384]{3,2,1,0:T(8,128)(2,1)S(1)}, u32[]{:S(2)}, u32[]{:S(2)}) collective-permute-start(bf16[1,2,256,384]{3,2,1,0:T(8,128)(2,1)S(1)} %collective-permute-done.5.refs_2_), channel_id=1, source_target_pairs={{0,2},{1,3},{2,0},{3,1},{4,6},{5,7},{6,4},{7,5},{8,10},{9,11},{10,... | collective-permute-start | bytes 1179656 | tf_op jit(solution)/shard_map/ppermute | solution.py:227
  38.0 8.6 %collective-permute-start.11 = (bf16[1,2,256,384]{3,2,1,0:T(8,128)(2,1)S(1)}, bf16[1,2,256,384]{3,2,1,0:T(8,128)(2,1)S(1)}, u32[]{:S(2)}, u32[]{:S(2)}) collective-permute-start(bf16[1,2,256,384]{3,2,1,0:T(8,128)(2,1)S(1)} %collective-permute-done.4.refs_1_), channel_id=1, source_target_pairs={{0,8},{8,0},{16,24},{24,16},{1,9},{9,1},{17,25},{25,17},{2,10},{10... | collective-permute-start | bytes 1179656 | tf_op jit(solution)/shard_map/ppermute | solution.py:227
  38.5 9.3 %collective-permute-start.12 = (bf16[1,2,256,384]{3,2,1,0:T(8,128)(2,1)S(1)}, bf16[1,2,256,384]{3,2,1,0:T(8,128)(2,1)S(1)}, u32[]{:S(2)}, u32[]{:S(2)}) collective-permute-start(bf16[1,2,256,384]{3,2,1,0:T(8,128)(2,1)S(1)} %collective-permute-done.4.refs_1_), channel_id=1, source_target_pairs={{0,16},{8,24},{16,0},{24,8},{1,17},{9,25},{17,1},{25,9},{2,18},{10... | collective-permute-start | bytes 1179656 | tf_op jit(solution)/shard_map/ppermute | solution.py:227
  40.0 7.7 %collective-permute-start.13 = (bf16[1,2,256,384]{3,2,1,0:T(8,128)(2,1)S(1)}, bf16[1,2,256,384]{3,2,1,0:T(8,128)(2,1)S(1)}, u32[]{:S(2)}, u32[]{:S(2)}) collective-permute-start(bf16[1,2,256,384]{3,2,1,0:T(8,128)(2,1)S(1)} %collective-permute-done.4.refs_1_), channel_id=1, source_target_pairs={{0,1},{1,0},{2,3},{3,2},{4,5},{5,4},{6,7},{7,6},{8,9},{9,8},{10,11... | collective-permute-start | bytes 1179656 | tf_op jit(solution)/shard_map/ppermute | solution.py:227
  40.0 7.7 %collective-permute-start.14 = (bf16[1,2,256,384]{3,2,1,0:T(8,128)(2,1)S(1)}, bf16[1,2,256,384]{3,2,1,0:T(8,128)(2,1)S(1)}, u32[]{:S(2)}, u32[]{:S(2)}) collective-permute-start(bf16[1,2,256,384]{3,2,1,0:T(8,128)(2,1)S(1)} %collective-permute-done.5.refs_2_), channel_id=1, source_target_pairs={{0,1},{1,0},{2,3},{3,2},{4,5},{5,4},{6,7},{7,6},{8,9},{9,8},{10,11... | collective-permute-start | bytes 1179656 | tf_op jit(solution)/shard_map/ppermute | solution.py:227
  47.9 20.0 %collective-permute-start.18 = (bf16[2,2,256,384]{3,2,1,0:T(8,128)(2,1)S(1)}, bf16[2,2,256,384]{3,2,1,0:T(8,128)(2,1)S(1)}, u32[]{:S(2)}, u32[]{:S(2)}) collective-permute-start(bf16[2,2,256,384]{3,2,1,0:T(8,128)(2,1)S(1)} %constant_dynamic-update-slice_fusion.5), channel_id=1, source_target_pairs={{0,8},{8,0},{16,24},{24,16},{1,9},{9,1},{17,25},{25,17},{2,10},{10... | collective-permute-start | bytes 2359304 | tf_op jit(solution)/shard_map/ppermute | solution.py:227
  48.5 19.7 %collective-permute-start.19 = (bf16[2,2,256,384]{3,2,1,0:T(8,128)(2,1)S(1)}, bf16[2,2,256,384]{3,2,1,0:T(8,128)(2,1)S(1)}, u32[]{:S(2)}, u32[]{:S(2)}) collective-permute-start(bf16[2,2,256,384]{3,2,1,0:T(8,128)(2,1)S(1)} %constant_dynamic-update-slice_fusion.5), channel_id=1, source_target_pairs={{0,16},{8,24},{16,0},{24,8},{1,17},{9,25},{17,1},{25,9},{2,18},{10... | collective-permute-start | bytes 2359304 | tf_op jit(solution)/shard_map/ppermute | solution.py:227
  50.2 17.9 %collective-permute-start.17 = (bf16[5,2,256,384]{3,2,1,0:T(8,128)(2,1)S(1)}, bf16[5,2,256,384]{3,2,1,0:T(8,128)(2,1)S(1)}, u32[]{:S(2)}, u32[]{:S(2)}) collective-permute-start(bf16[5,2,256,384]{3,2,1,0:T(8,128)(2,1)S(1)} %constant_dynamic-update-slice_fusion), channel_id=1, source_target_pairs={{0,1},{1,0},{2,3},{3,2},{4,5},{5,4},{6,7},{7,6},{8,9},{9,8},{10,11... | collective-permute-start | bytes 5898248 | tf_op jit(solution)/shard_map/ppermute | solution.py:227
  69.4 17.9 %collective-permute-start.22 = (bf16[2,256,384]{2,1,0:T(8,128)(2,1)S(1)}, bf16[2,256,384]{2,1,0:T(8,128)(2,1)S(1)}, u32[]{:S(2)}, u32[]{:S(2)}) collective-permute-start(bf16[2,256,384]{2,1,0:T(8,128)(2,1)S(1)} %slice.79), channel_id=1, source_target_pairs={{0,2},{1,3},{2,0},{3,1},{4,6},{5,7},{6,4},{7,5},{8,10},{9,11},{10,... | collective-permute-start | bytes 1179656 | tf_op jit(solution)/shard_map/ppermute | solution.py:227
  70.9 16.4 %collective-permute-start.23 = (bf16[1,2,384,384]{3,2,1,0:T(8,128)(2,1)S(1)}, bf16[1,2,384,384]{3,2,1,0:T(8,128)(2,1)S(1)}, u32[]{:S(2)}, u32[]{:S(2)}) collective-permute-start(bf16[1,2,384,384]{3,2,1,0:T(8,128)(2,1)S(1)} %pad_maximum_fusion.2), channel_id=1, source_target_pairs={{0,16},{8,24},{16,0},{24,8},{1,17},{9,25},{17,1},{25,9},{2,18},{10... | collective-permute-start | bytes 1769480 | tf_op jit(solution)/shard_map/ppermute | solution.py:227
  72.6 14.7 %collective-permute-start.24 = (bf16[1,2,384,384]{3,2,1,0:T(8,128)(2,1)S(1)}, bf16[1,2,384,384]{3,2,1,0:T(8,128)(2,1)S(1)}, u32[]{:S(2)}, u32[]{:S(2)}) collective-permute-start(bf16[1,2,384,384]{3,2,1,0:T(8,128)(2,1)S(1)} %pad_maximum_fusion.3), channel_id=1, source_target_pairs={{0,8},{8,0},{16,24},{24,16},{1,9},{9,1},{17,25},{25,17},{2,10},{10... | collective-permute-start | bytes 1769480 | tf_op jit(solution)/shard_map/ppermute | solution.py:227
  73.7 15.1 %collective-permute-start.25 = (bf16[2,256,384]{2,1,0:T(8,128)(2,1)S(1)}, bf16[2,256,384]{2,1,0:T(8,128)(2,1)S(1)}, u32[]{:S(2)}, u32[]{:S(2)}) collective-permute-start(bf16[2,256,384]{2,1,0:T(8,128)(2,1)S(1)} %slice.85), channel_id=1, source_target_pairs={{0,2},{1,3},{2,0},{3,1},{4,6},{5,7},{6,4},{7,5},{8,10},{9,11},{10,... | collective-permute-start | bytes 1179656 | tf_op jit(solution)/shard_map/ppermute | solution.py:227
  90.4 11.5 %collective-permute-start.27 = (bf16[256,384]{1,0:T(8,128)(2,1)S(1)}, bf16[256,384]{1,0:T(8,128)(2,1)S(1)}, u32[]{:S(2)}, u32[]{:S(2)}) collective-permute-start(bf16[256,384]{1,0:T(8,128)(2,1)S(1)} %fusion.18), channel_id=1, source_target_pairs={{0,4},{1,5},{2,6},{3,7},{4,0},{5,1},{6,2},{7,3},{8,12},{9,13},{10,... | collective-permute-start | bytes 589832 | tf_op jit(solution)/shard_map/ppermute | solution.py:227
  102.2 12.8 %collective-permute-start.28 = (bf16[256,384]{1,0:T(8,128)(2,1)S(1)}, bf16[256,384]{1,0:T(8,128)(2,1)S(1)}, u32[]{:S(2)}, u32[]{:S(2)}) collective-permute-start(bf16[256,384]{1,0:T(8,128)(2,1)S(1)} %fusion.19), channel_id=1, source_target_pairs={{0,4},{1,5},{2,6},{3,7},{4,0},{5,1},{6,2},{7,3},{8,12},{9,13},{10,... | collective-permute-start | bytes 589832 | tf_op jit(solution)/shard_map/ppermute | solution.py:227
  103.3 11.5 %collective-permute-start.32 = (f32[2,256]{1,0:T(2,128)S(1)}, f32[2,256]{1,0:T(2,128)S(1)}, u32[]{:S(2)}, u32[]{:S(2)}) collective-permute-start(f32[2,256]{1,0:T(2,128)S(1)} %add.98), channel_id=1, source_target_pairs={{0,6},{1,7},{2,4},{3,5},{4,2},{5,3},{6,0},{7,1},{8,14},{9,15},{10,... | collective-permute-start | bytes 6152 | tf_op jit(solution)/shard_map/ppermute | solution.py:227
  105.5 9.4 %collective-permute-start.31 = (f32[2,256]{1,0:T(2,128)S(1)}, f32[2,256]{1,0:T(2,128)S(1)}, u32[]{:S(2)}, u32[]{:S(2)}) collective-permute-start(f32[2,256]{1,0:T(2,128)S(1)} %add.98), channel_id=1, source_target_pairs={{0,4},{1,5},{2,6},{3,7},{4,0},{5,1},{6,2},{7,3},{8,12},{9,13},{10,... | collective-permute-start | bytes 6152 | tf_op jit(solution)/shard_map/ppermute | solution.py:227
  106.5 8.4 %collective-permute-start.30 = (f32[2,256]{1,0:T(2,128)S(1)}, f32[2,256]{1,0:T(2,128)S(1)}, u32[]{:S(2)}, u32[]{:S(2)}) collective-permute-start(f32[2,256]{1,0:T(2,128)S(1)} %add.98), channel_id=1, source_target_pairs={{0,2},{1,3},{2,0},{3,1},{4,6},{5,7},{6,4},{7,5},{8,10},{9,11},{10,... | collective-permute-start | bytes 6152 | tf_op jit(solution)/shard_map/ppermute | solution.py:227
  (37 other events, 272.7 us)

commit v2 on v1

--- a/solution.py
+++ b/solution.py
@@ -24,7 +24,7 @@
 
 
 def each_column_tile(length, body, loop):
-    tile = next((t for t in ((512,) * loop + (256, 128)) if length % t == 0), length)
+    tile = next((t for t in (256, 128) if length % t == 0), length)
     if not loop:
         for start in range(0, length, tile):
             body(slice(start, start + tile))
@@ -43,7 +43,7 @@
         out_specs=[pl.BlockSpec(memory_space=pltpu.VMEM)] * len(outs),
         out_shape=outs,
         scratch_shapes=scratch,
-        compiler_params=pltpu.CompilerParams(vmem_limit_bytes=9 * MIB),
+        compiler_params=pltpu.CompilerParams(vmem_limit_bytes=12 * MIB),
         cost_estimate=pl.CostEstimate(flops=int(weight * flops), bytes_accessed=0, transcendentals=0),
         name=name,
     )(*operands)
@@ -216,7 +216,7 @@
             pltpu.VMEM((2, tile, hidden), F32),
             pltpu.SemaphoreType.DMA((2,)),
         ],
-        compiler_params=pltpu.CompilerParams(vmem_limit_bytes=10 * MIB),
+        compiler_params=pltpu.CompilerParams(vmem_limit_bytes=12 * MIB),
         cost_estimate=pl.CostEstimate(flops=32 * tokens * height * hidden, bytes_accessed=0, transcendentals=0),
         name="weight_grads",
     )(*operands)
@@ -337,11 +337,9 @@
             ((1, early_s), (3, early_s), (2, far23_s), (3, far23_s)),
         )
         distant = chunk_products(spot, [left, right], up_weight, down_weight, height)
-        distant, half_dh, corner2, corner3 = together(distant, half_dh, corner2, corner3)
-        dh = dh[::2] + half_dh.astype(F32)
+        distant, half_dh, half_vel, corner2, corner3 = together(distant, half_dh, half_vel, corner2, corner3)
+        dh, velocity = dh[::2] + half_dh.astype(F32), velocity[::2] + half_vel.astype(F32)
         got_dh = along_z(dh[1].astype(BF16), 2)
-        distant, half_vel, corner2, corner3 = together(distant, half_vel, corner2, corner3)
-        velocity = velocity[::2] + half_vel.astype(F32)
         sent_vel = velocity[1].astype(BF16)
         corner1 = jnp.concatenate((corner2[:, :, rows:], corner3[:, :, rows:]), axis=2)
         late = jnp.concatenate((corner1, corner2[:, :, :rows], corner3[:, :, :rows]))
@@ -350,7 +348,7 @@
             ((0, corner0), (0, late), (1, late), (2, late)),
             ((4, early_s), (0, late_s), (1, late_s), (2, late_s)),
         )
-        last = chunk_products(spot, [corner], up_weight, down_weight, height, 0.02)
+        last = chunk_products(spot, [corner], up_weight, down_weight, height)
         last, got_dh, sent_vel = together(last, got_dh, sent_vel)
         dh = dh[0] + got_dh.astype(F32)
         dxhat = dh * (1.0 + scale)

time: 116 us -> 116 us (level)
  Pallas kernels: 41.3 us -> 42.5 us
  waiting for transfers between devices: 22.5 us -> 21.3 us
    ppermute x33, waiting for transfers between devices: 22.5 us -> 21.3 us  [swap(): return lax.ppermute(value, axis, [(i, i ^ bits) for i in range(size)])]
    pallas_call x5, Pallas kernels: 33 us -> 34.2 us  [call(): pl.pallas_call(kernel, in_specs=[pl.BlockSpec(memory_space=pltpu.SMEM)] +...]
  transfers between devices with their start and end apart: 33 -> 33, of which waited for: 13 -> 13; matrix products, arithmetic and copies ran while one was open for 5% -> 5% of each run, Pallas kernels for 36% -> 37%
where the time goes in v2:
time: 116 us
  Pallas kernels  42.5 us (37%)
  starting transfers between devices  32.4 us (28%)
  waiting for transfers between devices  21.3 us (18%)
  local copies, waits for them, and re-layouts  14.1 us (12%)
  other arithmetic  4.36 us (4%)
  between operations  1.27 us (1%)
    pallas_call x5, Pallas kernels, call(): pl.pallas_call(kernel, in_specs=[pl.BlockSpec(memory_space=pltpu.SMEM)] +...  34.2 us
    ppermute x33, starting transfers between devices, swap(): return lax.ppermute(value, axis, [(i, i ^ bits) for i in range(size)])  32.4 us
    ppermute x33, waiting for transfers between devices, swap(): return lax.ppermute(value, axis, [(i, i ^ bits) for i in range(size)])  21.3 us
    unnamed x53, local copies, waits for them, and re-layouts  9.58 us
    pallas_call x1, Pallas kernels, weight_grads(): pl.pallas_call(functools.partial(grad_kernel, len(chunks)), in_specs=[pl....  7.14 us
    gather x1, local copies, waits for them, and re-layouts, on_device(): cond = modulation.at[buckets].get(mode='promise_in_bounds')  4.09 us
  transfers between devices with their start and end apart: 33, of which 13 were waited for; matrix products, arithmetic and copies ran while one was open for 5% of the time, Pallas kernels for 37%

profile of v2, /device:TPU:0, one launch (start us, length us, event | category | flops | bytes accessed | tf_op | source)
XLA Modules:
  0.0 115.9 jit_solution(16328797926528242934)
XLA Ops:
  3.1 5.0 %collective-permute-start.3 = (f32[2,256]{1,0:T(2,128)S(1)}, f32[2,256]{1,0:T(2,128)S(1)}, u32[]{:S(2)}, u32[]{:S(2)}) collective-permute-start(f32[2,256]{1,0:T(2,128)S(1)} %fusion.22), channel_id=1, source_target_pairs={{0,6},{1,7},{2,4},{3,5},{4,2},{5,3},{6,0},{7,1},{8,14},{9,15},{10,... | collective-permute-start | bytes 6152 | tf_op jit(solution)/shard_map/ppermute | solution.py:227
  8.7 4.1 %gather_fusion = f32[256,3,384]{2,0,1:T(8,128)S(1)} fusion(f32[1000,3,384]{2,0,1:T(8,128)} %param.8, s32[1024]{0:T(1024)S(1)} %pad_clamp_fusion), kind=kCustom, calls=%fused_computation | custom fusion | bytes 2360320 | tf_op jit(solution)/shard_map/gather | solution.py:285
  13.9 1.7 %collective-permute-start.6 = (bf16[1,2,256,384]{3,2,1,0:T(8,128)(2,1)S(1)}, bf16[1,2,256,384]{3,2,1,0:T(8,128)(2,1)S(1)}, u32[]{:S(2)}, u32[]{:S(2)}) collective-permute-start(bf16[1,2,256,384]{3,2,1,0:T(8,128)(2,1)S(1)} %maximum_bitcast_fusion.refs_0_), channel_id=1, source_target_pairs={{0,8},{8,0},{16,24},{24,16},{1,9},{9,1},{17,25},{25,17},{2,10},{10... | collective-permute-start | bytes 1179656 | tf_op jit(solution)/shard_map/ppermute | solution.py:227
  16.8 2.9 %collective-permute-start.5 = (bf16[1,2,256,384]{3,2,1,0:T(8,128)(2,1)S(1)}, bf16[1,2,256,384]{3,2,1,0:T(8,128)(2,1)S(1)}, u32[]{:S(2)}, u32[]{:S(2)}) collective-permute-start(bf16[1,2,256,384]{3,2,1,0:T(8,128)(2,1)S(1)} %maximum_bitcast_fusion.refs_0_), channel_id=1, source_target_pairs={{0,4},{1,5},{2,6},{3,7},{4,0},{5,1},{6,2},{7,3},{8,12},{9,13},{10,... | collective-permute-start | bytes 1179656 | tf_op jit(solution)/shard_map/ppermute | solution.py:227
  19.8 1.5 %collective-permute-start.7 = (bf16[1,2,256,384]{3,2,1,0:T(8,128)(2,1)S(1)}, bf16[1,2,256,384]{3,2,1,0:T(8,128)(2,1)S(1)}, u32[]{:S(2)}, u32[]{:S(2)}) collective-permute-start(bf16[1,2,256,384]{3,2,1,0:T(8,128)(2,1)S(1)} %maximum_bitcast_fusion.refs_0_), channel_id=1, source_target_pairs={{0,16},{8,24},{16,0},{24,8},{1,17},{9,25},{17,1},{25,9},{2,18},{10... | collective-permute-start | bytes 1179656 | tf_op jit(solution)/shard_map/ppermute | solution.py:227
  21.3 3.3 %collective-permute-done.6.refs_0_ = bf16[1,2,256,384]{3,2,1,0:T(8,128)(2,1)S(1)} collective-permute-done((bf16[1,2,256,384]{3,2,1,0:T(8,128)(2,1)S(1)}, bf16[1,2,256,384]{3,2,1,0:T(8,128)(2,1)S(1)}, u32[]{:S(2)}, u32[]{:S(2)}) %collective-permute-start.6) | collective-permute-done | bytes 393248 | tf_op jit(solution)/shard_map/ppermute | solution.py:227
  24.6 1.5 %collective-permute-start.8 = (bf16[1,2,256,384]{3,2,1,0:T(8,128)(2,1)S(1)}, bf16[1,2,256,384]{3,2,1,0:T(8,128)(2,1)S(1)}, u32[]{:S(2)}, u32[]{:S(2)}) collective-permute-start(bf16[1,2,256,384]{3,2,1,0:T(8,128)(2,1)S(1)} %collective-permute-done.6.refs_0_), channel_id=1, source_target_pairs={{0,16},{8,24},{16,0},{24,8},{1,17},{9,25},{17,1},{25,9},{2,18},{10... | collective-permute-start | bytes 1179656 | tf_op jit(solution)/shard_map/ppermute | solution.py:227
  26.2 3.7 %copy-done = bf16[3072,1536]{1,0:T(8,128)(2,1)S(1)} copy-done((bf16[3072,1536]{1,0:T(8,128)(2,1)S(1)}, bf16[3072,1536]{1,0:T(8,128)(2,1)}, u32[]{:S(2)}) %copy-start) | copy-done | bytes 9437208
  29.8 3.7 %copy-done.1 = bf16[3072,1536]{1,0:T(8,128)(2,1)S(1)} copy-done((bf16[3072,1536]{1,0:T(8,128)(2,1)S(1)}, bf16[3072,1536]{1,0:T(8,128)(2,1)}, u32[]{:S(2)}) %copy-start.1) | copy-done | bytes 9437208
  34.7 1.6 %collective-permute-done.5.refs_2_ = bf16[1,2,256,384]{3,2,1,0:T(8,128)(2,1)S(1)} collective-permute-done((bf16[1,2,256,384]{3,2,1,0:T(8,128)(2,1)S(1)}, bf16[1,2,256,384]{3,2,1,0:T(8,128)(2,1)S(1)}, u32[]{:S(2)}, u32[]{:S(2)}) %collective-permute-start.5) | collective-permute-done | bytes 393248 | tf_op jit(solution)/shard_map/ppermute | solution.py:227
  38.5 1.5 %collective-permute-start.12 = (bf16[1,2,256,384]{3,2,1,0:T(8,128)(2,1)S(1)}, bf16[1,2,256,384]{3,2,1,0:T(8,128)(2,1)S(1)}, u32[]{:S(2)}, u32[]{:S(2)}) collective-permute-start(bf16[1,2,256,384]{3,2,1,0:T(8,128)(2,1)S(1)} %collective-permute-done.4.refs_1_), channel_id=1, source_target_pairs={{0,16},{8,24},{16,0},{24,8},{1,17},{9,25},{17,1},{25,9},{2,18},{10... | collective-permute-start | bytes 1179656 | tf_op jit(solution)/shard_map/ppermute | solution.py:227
  40.7 5.5 %collective-permute-done.10.refs_3_ = bf16[1,2,256,384]{3,2,1,0:T(8,128)(2,1)S(1)} collective-permute-done((bf16[1,2,256,384]{3,2,1,0:T(8,128)(2,1)S(1)}, bf16[1,2,256,384]{3,2,1,0:T(8,128)(2,1)S(1)}, u32[]{:S(2)}, u32[]{:S(2)}) %collective-permute-start.10) | collective-permute-done | bytes 393248 | tf_op jit(solution)/shard_map/ppermute | solution.py:227
  48.5 1.5 %collective-permute-start.19 = (bf16[2,2,256,384]{3,2,1,0:T(8,128)(2,1)S(1)}, bf16[2,2,256,384]{3,2,1,0:T(8,128)(2,1)S(1)}, u32[]{:S(2)}, u32[]{:S(2)}) collective-permute-start(bf16[2,2,256,384]{3,2,1,0:T(8,128)(2,1)S(1)} %constant_dynamic-update-slice_fusion.5), channel_id=1, source_target_pairs={{0,16},{8,24},{16,0},{24,8},{1,17},{9,25},{17,1},{25,9},{2,18},{10... | collective-permute-start | bytes 2359304 | tf_op jit(solution)/shard_map/ppermute | solution.py:227
  50.4 7.2 %chunk_products.3 = (bf16[256,1536]{1,0:T(8,128)(2,1)S(1)}, bf16[256,1536]{1,0:T(8,128)(2,1)S(1)}, bf16[256,768]{1,0:T(8,128)(2,1)S(1)}, bf16[256,768]{1,0:T(8,128)(2,1)S(1)}) custom-call(s32[3]{0:T(128)S(1)} %bring_weights.1.spot.left_spot, bf16[1,2,256,384]{3,2,1,0:T(8,128)(2,1)S(1)} %maximum_bitcast_fusion.refs_0_, ...), custom_call_target="tpu_custom_call" | custom-call | flops 38654705664 | tf_op jit(solution)/shard_map/chunk_products/pallas_call | solution.py:39
  57.6 3.6 %dh_share.1 = (bf16[4,256,384]{2,1,0:T(8,128)(2,1)S(1)}, bf16[4,256,384]{2,1,0:T(8,128)(2,1)S(1)}) custom-call(s32[3]{0:T(128)S(1)} %bring_weights.1.spot.left_spot, bf16[256,1536]{1,0:T(8,128)(2,1)S(1)} %get-tuple-element.108.left.refs_0_, bf16[3072,1536]{1,0:T(8,128)(2,1)S(1)} %bitcast.56), custom_call_target="tpu_custom_call" | custom-call | flops 19327352832 | tf_op jit(solution)/shard_map/dh_share/pallas_call | solution.py:39
  61.7 3.3 %velocity_share.1 = (bf16[4,256,384]{2,1,0:T(8,128)(2,1)S(1)}, bf16[4,256,384]{2,1,0:T(8,128)(2,1)S(1)}) custom-call(s32[3]{0:T(128)S(1)} %bring_weights.1.spot.left_spot, bf16[256,1536]{1,0:T(8,128)(2,1)S(1)} %get-tuple-element.109.left.refs_1_, bf16[3072,1536]{1,0:T(8,128)(2,1)S(1)} %copy-done.2), custom_call_target="tpu_custom_call" | custom-call | flops 19327352832 | tf_op jit(solution)/shard_map/velocity_share/pallas_call | solution.py:39
  65.0 2.9 %collective-permute-done.18.refs_2_.refs_3_ = bf16[2,2,256,384]{3,2,1,0:T(8,128)(2,1)S(1)} collective-permute-done((bf16[2,2,256,384]{3,2,1,0:T(8,128)(2,1)S(1)}, bf16[2,2,256,384]{3,2,1,0:T(8,128)(2,1)S(1)}, u32[]{:S(2)}, u32[]{:S(2)}) %collective-permute-start.18) | collective-permute-done | bytes 786464 | tf_op jit(solution)/shard_map/ppermute | solution.py:227
  69.4 1.5 %collective-permute-start.22 = (bf16[2,256,384]{2,1,0:T(8,128)(2,1)S(1)}, bf16[2,256,384]{2,1,0:T(8,128)(2,1)S(1)}, u32[]{:S(2)}, u32[]{:S(2)}) collective-permute-start(bf16[2,256,384]{2,1,0:T(8,128)(2,1)S(1)} %slice.79), channel_id=1, source_target_pairs={{0,2},{1,3},{2,0},{3,1},{4,6},{5,7},{6,4},{7,5},{8,10},{9,11},{10,... | collective-permute-start | bytes 1179656 | tf_op jit(solution)/shard_map/ppermute | solution.py:227
  70.9 1.6 %collective-permute-start.24 = (bf16[1,2,384,384]{3,2,1,0:T(8,128)(2,1)S(1)}, bf16[1,2,384,384]{3,2,1,0:T(8,128)(2,1)S(1)}, u32[]{:S(2)}, u32[]{:S(2)}) collective-permute-start(bf16[1,2,384,384]{3,2,1,0:T(8,128)(2,1)S(1)} %pad_maximum_fusion.2), channel_id=1, source_target_pairs={{0,16},{8,24},{16,0},{24,8},{1,17},{9,25},{17,1},{25,9},{2,18},{10... | collective-permute-start | bytes 1769480 | tf_op jit(solution)/shard_map/ppermute | solution.py:227
  75.1 13.3 %chunk_products.4 = (bf16[512,1536]{1,0:T(8,128)(2,1)S(1)}, bf16[512,1536]{1,0:T(8,128)(2,1)S(1)}, bf16[512,768]{1,0:T(8,128)(2,1)S(1)}, bf16[512,768]{1,0:T(8,128)(2,1)S(1)}) custom-call(s32[3]{0:T(128)S(1)} %bring_weights.1.spot.left_spot, bf16[1,2,256,384]{3,2,1,0:T(8,128)(2,1)S(1)} %collective-permute-done.6.refs_0_, ...), custom_call_target="tpu_custom_call" | custom-call | flops 77309411328 | tf_op jit(solution)/shard_map/chunk_products/pallas_call | solution.py:39
  92.0 6.8 %chunk_products.5 = (bf16[256,1536]{1,0:T(8,128)(2,1)S(1)}, bf16[256,1536]{1,0:T(8,128)(2,1)S(1)}, bf16[256,768]{1,0:T(8,128)(2,1)S(1)}, bf16[256,768]{1,0:T(8,128)(2,1)S(1)}) custom-call(s32[3]{0:T(128)S(1)} %bring_weights.1.spot.left_spot, bf16[1,2,256,384]{3,2,1,0:T(8,128)(2,1)S(1)} %collective-permute-done.8.refs_0_, ...), custom_call_target="tpu_custom_call" | custom-call | flops 38654705664 | tf_op jit(solution)/shard_map/chunk_products/pallas_call | solution.py:39
  98.8 3.0 %collective-permute-done.27 = bf16[256,384]{1,0:T(8,128)(2,1)S(1)} collective-permute-done((bf16[256,384]{1,0:T(8,128)(2,1)S(1)}, bf16[256,384]{1,0:T(8,128)(2,1)S(1)}, u32[]{:S(2)}, u32[]{:S(2)}) %collective-permute-start.27) | collective-permute-done | bytes 196640 | tf_op jit(solution)/shard_map/ppermute | solution.py:227
  103.4 2.1 %collective-permute-start.32 = (f32[2,256]{1,0:T(2,128)S(1)}, f32[2,256]{1,0:T(2,128)S(1)}, u32[]{:S(2)}, u32[]{:S(2)}) collective-permute-start(f32[2,256]{1,0:T(2,128)S(1)} %add.98), channel_id=1, source_target_pairs={{0,6},{1,7},{2,4},{3,5},{4,2},{5,3},{6,0},{7,1},{8,14},{9,15},{10,... | collective-permute-start | bytes 6152 | tf_op jit(solution)/shard_map/ppermute | solution.py:227
  107.7 7.1 %weight_grads.1 = (f32[768,1536]{1,0:T(8,128)}, f32[768,1536]{1,0:T(8,128)}) custom-call(bf16[256,1536]{1,0:T(8,128)(2,1)S(1)} %get-tuple-element.108.left.refs_0_, bf16[256,1536]{1,0:T(8,128)(2,1)S(1)} %get-tuple-element.109.left.refs_1_, bf16[256,768]{1,0:T(8,128)(2,1)S(1)} %get-tuple-element.110.refs_2_, bf16[256,768]{1,0:T(8,128)(2,1)S(1)} %get-tuple-element.111.refs_3_, ...), custom_call_target="tpu_custom_call" | custom-call | flops 38654705664 | tf_op jit(solution)/shard_map/weight_grads/pallas_call | solution.py:208
  (148 shorter events, 24.7 us)
Async XLA Ops:
  3.1 9.8 %collective-permute-start.3 = (f32[2,256]{1,0:T(2,128)S(1)}, f32[2,256]{1,0:T(2,128)S(1)}, u32[]{:S(2)}, u32[]{:S(2)}) collective-permute-start(f32[2,256]{1,0:T(2,128)S(1)} %fusion.22), channel_id=1, source_target_pairs={{0,6},{1,7},{2,4},{3,5},{4,2},{5,3},{6,0},{7,1},{8,14},{9,15},{10,... | collective-permute-start | bytes 6152 | tf_op jit(solution)/shard_map/ppermute | solution.py:227
  13.9 10.7 %collective-permute-start.6 = (bf16[1,2,256,384]{3,2,1,0:T(8,128)(2,1)S(1)}, bf16[1,2,256,384]{3,2,1,0:T(8,128)(2,1)S(1)}, u32[]{:S(2)}, u32[]{:S(2)}) collective-permute-start(bf16[1,2,256,384]{3,2,1,0:T(8,128)(2,1)S(1)} %maximum_bitcast_fusion.refs_0_), channel_id=1, source_target_pairs={{0,8},{8,0},{16,24},{24,16},{1,9},{9,1},{17,25},{25,17},{2,10},{10... | collective-permute-start | bytes 1179656 | tf_op jit(solution)/shard_map/ppermute | solution.py:227
  15.6 19.1 %collective-permute-start.4 = (bf16[1,2,256,384]{3,2,1,0:T(8,128)(2,1)S(1)}, bf16[1,2,256,384]{3,2,1,0:T(8,128)(2,1)S(1)}, u32[]{:S(2)}, u32[]{:S(2)}) collective-permute-start(bf16[1,2,256,384]{3,2,1,0:T(8,128)(2,1)S(1)} %maximum_bitcast_fusion.refs_0_), channel_id=1, source_target_pairs={{0,2},{1,3},{2,0},{3,1},{4,6},{5,7},{6,4},{7,5},{8,10},{9,11},{10,... | collective-permute-start | bytes 1179656 | tf_op jit(solution)/shard_map/ppermute | solution.py:227
  16.8 19.4 %collective-permute-start.5 = (bf16[1,2,256,384]{3,2,1,0:T(8,128)(2,1)S(1)}, bf16[1,2,256,384]{3,2,1,0:T(8,128)(2,1)S(1)}, u32[]{:S(2)}, u32[]{:S(2)}) collective-permute-start(bf16[1,2,256,384]{3,2,1,0:T(8,128)(2,1)S(1)} %maximum_bitcast_fusion.refs_0_), channel_id=1, source_target_pairs={{0,4},{1,5},{2,6},{3,7},{4,0},{5,1},{6,2},{7,3},{8,12},{9,13},{10,... | collective-permute-start | bytes 1179656 | tf_op jit(solution)/shard_map/ppermute | solution.py:227
  19.8 16.5 %collective-permute-start.7 = (bf16[1,2,256,384]{3,2,1,0:T(8,128)(2,1)S(1)}, bf16[1,2,256,384]{3,2,1,0:T(8,128)(2,1)S(1)}, u32[]{:S(2)}, u32[]{:S(2)}) collective-permute-start(bf16[1,2,256,384]{3,2,1,0:T(8,128)(2,1)S(1)} %maximum_bitcast_fusion.refs_0_), channel_id=1, source_target_pairs={{0,16},{8,24},{16,0},{24,8},{1,17},{9,25},{17,1},{25,9},{2,18},{10... | collective-permute-start | bytes 1179656 | tf_op jit(solution)/shard_map/ppermute | solution.py:227
  21.3 15.0 %collective-permute-start.9 = (bf16[1,2,256,384]{3,2,1,0:T(8,128)(2,1)S(1)}, bf16[1,2,256,384]{3,2,1,0:T(8,128)(2,1)}, u32[]{:S(2)}, u32[]{:S(2)}) collective-permute-start(bf16[1,2,256,384]{3,2,1,0:T(8,128)(2,1)S(1)} %maximum_bitcast_fusion.refs_0_), channel_id=1, source_target_pairs={{0,1},{1,0},{2,3},{3,2},{4,5},{5,4},{6,7},{7,6},{8,9},{9,8},{10,11... | collective-permute-start | bytes 1179656 | tf_op jit(solution)/shard_map/ppermute | solution.py:227
  24.6 13.1 %collective-permute-start.8 = (bf16[1,2,256,384]{3,2,1,0:T(8,128)(2,1)S(1)}, bf16[1,2,256,384]{3,2,1,0:T(8,128)(2,1)S(1)}, u32[]{:S(2)}, u32[]{:S(2)}) collective-permute-start(bf16[1,2,256,384]{3,2,1,0:T(8,128)(2,1)S(1)} %collective-permute-done.6.refs_0_), channel_id=1, source_target_pairs={{0,16},{8,24},{16,0},{24,8},{1,17},{9,25},{17,1},{25,9},{2,18},{10... | collective-permute-start | bytes 1179656 | tf_op jit(solution)/shard_map/ppermute | solution.py:227
  37.7 8.6 %collective-permute-start.10 = (bf16[1,2,256,384]{3,2,1,0:T(8,128)(2,1)S(1)}, bf16[1,2,256,384]{3,2,1,0:T(8,128)(2,1)S(1)}, u32[]{:S(2)}, u32[]{:S(2)}) collective-permute-start(bf16[1,2,256,384]{3,2,1,0:T(8,128)(2,1)S(1)} %collective-permute-done.5.refs_2_), channel_id=1, source_target_pairs={{0,2},{1,3},{2,0},{3,1},{4,6},{5,7},{6,4},{7,5},{8,10},{9,11},{10,... | collective-permute-start | bytes 1179656 | tf_op jit(solution)/shard_map/ppermute | solution.py:227
  38.0 8.6 %collective-permute-start.11 = (bf16[1,2,256,384]{3,2,1,0:T(8,128)(2,1)S(1)}, bf16[1,2,256,384]{3,2,1,0:T(8,128)(2,1)S(1)}, u32[]{:S(2)}, u32[]{:S(2)}) collective-permute-start(bf16[1,2,256,384]{3,2,1,0:T(8,128)(2,1)S(1)} %collective-permute-done.4.refs_1_), channel_id=1, source_target_pairs={{0,8},{8,0},{16,24},{24,16},{1,9},{9,1},{17,25},{25,17},{2,10},{10... | collective-permute-start | bytes 1179656 | tf_op jit(solution)/shard_map/ppermute | solution.py:227
  38.5 9.3 %collective-permute-start.12 = (bf16[1,2,256,384]{3,2,1,0:T(8,128)(2,1)S(1)}, bf16[1,2,256,384]{3,2,1,0:T(8,128)(2,1)S(1)}, u32[]{:S(2)}, u32[]{:S(2)}) collective-permute-start(bf16[1,2,256,384]{3,2,1,0:T(8,128)(2,1)S(1)} %collective-permute-done.4.refs_1_), channel_id=1, source_target_pairs={{0,16},{8,24},{16,0},{24,8},{1,17},{9,25},{17,1},{25,9},{2,18},{10... | collective-permute-start | bytes 1179656 | tf_op jit(solution)/shard_map/ppermute | solution.py:227
  40.0 7.7 %collective-permute-start.13 = (bf16[1,2,256,384]{3,2,1,0:T(8,128)(2,1)S(1)}, bf16[1,2,256,384]{3,2,1,0:T(8,128)(2,1)S(1)}, u32[]{:S(2)}, u32[]{:S(2)}) collective-permute-start(bf16[1,2,256,384]{3,2,1,0:T(8,128)(2,1)S(1)} %collective-permute-done.4.refs_1_), channel_id=1, source_target_pairs={{0,1},{1,0},{2,3},{3,2},{4,5},{5,4},{6,7},{7,6},{8,9},{9,8},{10,11... | collective-permute-start | bytes 1179656 | tf_op jit(solution)/shard_map/ppermute | solution.py:227
  40.0 7.7 %collective-permute-start.14 = (bf16[1,2,256,384]{3,2,1,0:T(8,128)(2,1)S(1)}, bf16[1,2,256,384]{3,2,1,0:T(8,128)(2,1)S(1)}, u32[]{:S(2)}, u32[]{:S(2)}) collective-permute-start(bf16[1,2,256,384]{3,2,1,0:T(8,128)(2,1)S(1)} %collective-permute-done.5.refs_2_), channel_id=1, source_target_pairs={{0,1},{1,0},{2,3},{3,2},{4,5},{5,4},{6,7},{7,6},{8,9},{9,8},{10,11... | collective-permute-start | bytes 1179656 | tf_op jit(solution)/shard_map/ppermute | solution.py:227
  47.9 20.0 %collective-permute-start.18 = (bf16[2,2,256,384]{3,2,1,0:T(8,128)(2,1)S(1)}, bf16[2,2,256,384]{3,2,1,0:T(8,128)(2,1)S(1)}, u32[]{:S(2)}, u32[]{:S(2)}) collective-permute-start(bf16[2,2,256,384]{3,2,1,0:T(8,128)(2,1)S(1)} %constant_dynamic-update-slice_fusion.5), channel_id=1, source_target_pairs={{0,8},{8,0},{16,24},{24,16},{1,9},{9,1},{17,25},{25,17},{2,10},{10... | collective-permute-start | bytes 2359304 | tf_op jit(solution)/shard_map/ppermute | solution.py:227
  48.5 19.7 %collective-permute-start.19 = (bf16[2,2,256,384]{3,2,1,0:T(8,128)(2,1)S(1)}, bf16[2,2,256,384]{3,2,1,0:T(8,128)(2,1)S(1)}, u32[]{:S(2)}, u32[]{:S(2)}) collective-permute-start(bf16[2,2,256,384]{3,2,1,0:T(8,128)(2,1)S(1)} %constant_dynamic-update-slice_fusion.5), channel_id=1, source_target_pairs={{0,16},{8,24},{16,0},{24,8},{1,17},{9,25},{17,1},{25,9},{2,18},{10... | collective-permute-start | bytes 2359304 | tf_op jit(solution)/shard_map/ppermute | solution.py:227
  50.2 17.9 %collective-permute-start.17 = (bf16[5,2,256,384]{3,2,1,0:T(8,128)(2,1)S(1)}, bf16[5,2,256,384]{3,2,1,0:T(8,128)(2,1)S(1)}, u32[]{:S(2)}, u32[]{:S(2)}) collective-permute-start(bf16[5,2,256,384]{3,2,1,0:T(8,128)(2,1)S(1)} %constant_dynamic-update-slice_fusion), channel_id=1, source_target_pairs={{0,1},{1,0},{2,3},{3,2},{4,5},{5,4},{6,7},{7,6},{8,9},{9,8},{10,11... | collective-permute-start | bytes 5898248 | tf_op jit(solution)/shard_map/ppermute | solution.py:227
  69.4 19.1 %collective-permute-start.22 = (bf16[2,256,384]{2,1,0:T(8,128)(2,1)S(1)}, bf16[2,256,384]{2,1,0:T(8,128)(2,1)S(1)}, u32[]{:S(2)}, u32[]{:S(2)}) collective-permute-start(bf16[2,256,384]{2,1,0:T(8,128)(2,1)S(1)} %slice.79), channel_id=1, source_target_pairs={{0,2},{1,3},{2,0},{3,1},{4,6},{5,7},{6,4},{7,5},{8,10},{9,11},{10,... | collective-permute-start | bytes 1179656 | tf_op jit(solution)/shard_map/ppermute | solution.py:227
  70.9 17.5 %collective-permute-start.24 = (bf16[1,2,384,384]{3,2,1,0:T(8,128)(2,1)S(1)}, bf16[1,2,384,384]{3,2,1,0:T(8,128)(2,1)S(1)}, u32[]{:S(2)}, u32[]{:S(2)}) collective-permute-start(bf16[1,2,384,384]{3,2,1,0:T(8,128)(2,1)S(1)} %pad_maximum_fusion.2), channel_id=1, source_target_pairs={{0,16},{8,24},{16,0},{24,8},{1,17},{9,25},{17,1},{25,9},{2,18},{10... | collective-permute-start | bytes 1769480 | tf_op jit(solution)/shard_map/ppermute | solution.py:227
  72.6 15.9 %collective-permute-start.25 = (bf16[1,2,384,384]{3,2,1,0:T(8,128)(2,1)S(1)}, bf16[1,2,384,384]{3,2,1,0:T(8,128)(2,1)S(1)}, u32[]{:S(2)}, u32[]{:S(2)}) collective-permute-start(bf16[1,2,384,384]{3,2,1,0:T(8,128)(2,1)S(1)} %pad_maximum_fusion.3), channel_id=1, source_target_pairs={{0,8},{8,0},{16,24},{24,16},{1,9},{9,1},{17,25},{25,17},{2,10},{10... | collective-permute-start | bytes 1769480 | tf_op jit(solution)/shard_map/ppermute | solution.py:227
  73.7 15.1 %collective-permute-start.23 = (bf16[2,256,384]{2,1,0:T(8,128)(2,1)S(1)}, bf16[2,256,384]{2,1,0:T(8,128)(2,1)S(1)}, u32[]{:S(2)}, u32[]{:S(2)}) collective-permute-start(bf16[2,256,384]{2,1,0:T(8,128)(2,1)S(1)} %slice.80), channel_id=1, source_target_pairs={{0,2},{1,3},{2,0},{3,1},{4,6},{5,7},{6,4},{7,5},{8,10},{9,11},{10,... | collective-permute-start | bytes 1179656 | tf_op jit(solution)/shard_map/ppermute | solution.py:227
  90.4 11.5 %collective-permute-start.27 = (bf16[256,384]{1,0:T(8,128)(2,1)S(1)}, bf16[256,384]{1,0:T(8,128)(2,1)S(1)}, u32[]{:S(2)}, u32[]{:S(2)}) collective-permute-start(bf16[256,384]{1,0:T(8,128)(2,1)S(1)} %fusion.18), channel_id=1, source_target_pairs={{0,4},{1,5},{2,6},{3,7},{4,0},{5,1},{6,2},{7,3},{8,12},{9,13},{10,... | collective-permute-start | bytes 589832 | tf_op jit(solution)/shard_map/ppermute | solution.py:227
  102.2 12.8 %collective-permute-start.28 = (bf16[256,384]{1,0:T(8,128)(2,1)S(1)}, bf16[256,384]{1,0:T(8,128)(2,1)S(1)}, u32[]{:S(2)}, u32[]{:S(2)}) collective-permute-start(bf16[256,384]{1,0:T(8,128)(2,1)S(1)} %fusion.19), channel_id=1, source_target_pairs={{0,4},{1,5},{2,6},{3,7},{4,0},{5,1},{6,2},{7,3},{8,12},{9,13},{10,... | collective-permute-start | bytes 589832 | tf_op jit(solution)/shard_map/ppermute | solution.py:227
  103.4 11.5 %collective-permute-start.32 = (f32[2,256]{1,0:T(2,128)S(1)}, f32[2,256]{1,0:T(2,128)S(1)}, u32[]{:S(2)}, u32[]{:S(2)}) collective-permute-start(f32[2,256]{1,0:T(2,128)S(1)} %add.98), channel_id=1, source_target_pairs={{0,6},{1,7},{2,4},{3,5},{4,2},{5,3},{6,0},{7,1},{8,14},{9,15},{10,... | collective-permute-start | bytes 6152 | tf_op jit(solution)/shard_map/ppermute | solution.py:227
  105.5 9.4 %collective-permute-start.31 = (f32[2,256]{1,0:T(2,128)S(1)}, f32[2,256]{1,0:T(2,128)S(1)}, u32[]{:S(2)}, u32[]{:S(2)}) collective-permute-start(f32[2,256]{1,0:T(2,128)S(1)} %add.98), channel_id=1, source_target_pairs={{0,4},{1,5},{2,6},{3,7},{4,0},{5,1},{6,2},{7,3},{8,12},{9,13},{10,... | collective-permute-start | bytes 6152 | tf_op jit(solution)/shard_map/ppermute | solution.py:227
  106.5 8.4 %collective-permute-start.30 = (f32[2,256]{1,0:T(2,128)S(1)}, f32[2,256]{1,0:T(2,128)S(1)}, u32[]{:S(2)}, u32[]{:S(2)}) collective-permute-start(f32[2,256]{1,0:T(2,128)S(1)} %add.98), channel_id=1, source_target_pairs={{0,2},{1,3},{2,0},{3,1},{4,6},{5,7},{6,4},{7,5},{8,10},{9,11},{10,... | collective-permute-start | bytes 6152 | tf_op jit(solution)/shard_map/ppermute | solution.py:227
  (37 other events, 272.6 us)
